TPU v7x, 128 devices: a whole 4x4x4 slice. The times are simulated.
128 devices in a mesh: seq: 8 (over z, core), head: 16 (over y, x).
Axes of the slice: x: 4, y: 4, z: 4, core: 2. Of those that a mesh axis runs over, the one named last changes fastest.
Arguments:
- tokens: bfloat16 [2, 2048, 2048], P(None, 'seq', 'head'), may hold values from -6 to 6
- attn_gain: float32 [2048], replicated, may hold values from 0.1 to 1.9
- w_query: bfloat16 [2048, 4096], P(None, 'head'), may hold values from -0.125 to 0.125
- w_key: bfloat16 [2048, 4096], P(None, 'head'), may hold values from -0.125 to 0.125
- w_value: bfloat16 [2048, 4096], P(None, 'head'), may hold values from -0.125 to 0.125
- w_gate: bfloat16 [2048, 4096], P(None, 'head'), may hold values from -0.125 to 0.125
- head_gain: float32 [4096], P('head'), may hold values from 0.1 to 1.9
- w_out: bfloat16 [4096, 2048], P('head'), may hold values from -0.09375 to 0.09375
- moe_gain: float32 [2048], replicated, may hold values from 0.1 to 1.9
- w_router: bfloat16 [2048, 128], replicated, may hold values from -0.125 to 0.125
- expert_picks: int32 [8, 512, 8], P('seq', 'head'), may hold values from 0 to 127, all different within a row; in each aligned block of 32 rows (0 to 31, 32 to 63, ..., all dimensions but the last counted through in order) at most 3 rows name the same one
- exp_gate: bfloat16 [128, 2048, 768], P(('seq', 'head')), may hold values from -0.125 to 0.125
- exp_up: bfloat16 [128, 2048, 768], P(('seq', 'head')), may hold values from -0.125 to 0.125
- exp_down: bfloat16 [128, 768, 2048], P(('seq', 'head')), may hold values from -0.21875 to 0.21875
Outputs:
- layer_out: float32 [8, 512, 2048], P('seq', 'head')
Inputs may be any that keep to these rules, and one draw needn't show every extreme that they name: `expert_picks`: each row names 8 different experts. In each aligned block of 32 rows no expert is named by more than 3 rows, a bound that some block reaches.
All inputs are finite; a program needn't handle non-finite values.
Results may differ from a plain program's by a relative error of at most 0.007.
Values may be sent and summed in bfloat16 or wider, within the bound.
A program may use at most 64 MiB of HBM per device.

v0:
```python
import jax
import jax.numpy as jnp
from jax import lax
from jax.sharding import PartitionSpec as P

DH = 128
BLOCK = 256


epsilon = 1e-06


def laid_out(pieces, dim):
    pieces = jnp.moveaxis(pieces, 0, dim)
    dims = pieces.shape
    return pieces.reshape(*dims[:dim], dims[dim] * dims[dim + 1], *dims[dim + 2 :])


def from_everyone(value, axis):
    copies = jnp.broadcast_to(value, (lax.axis_size(axis), *value.shape))
    return lax.all_to_all(copies, axis, split_axis=0, concat_axis=0, tiled=True)


def gather_directly(value, axis, dim):
    return laid_out(from_everyone(value, axis), dim)


def split_up(value, dim, devices):
    before, after = (value.shape[:dim], value.shape[dim + 1 :])
    return jnp.moveaxis(value.reshape(*before, devices, -1, *after), dim, 0)


def summed_on_arrival(value, axis, dim):
    pieces = split_up(value, dim, lax.axis_size(axis))
    arrived = lax.all_to_all(pieces, axis, split_axis=0, concat_axis=0, tiled=True)
    return arrived.astype(jnp.float32).sum(axis=0)


def exchange_both(value, axis, axes, splits, concats):
    sizes = [lax.axis_size(a) for a in axes]
    pieces = split_up(value, splits[0], sizes[0])
    pieces = jnp.moveaxis(split_up(pieces, splits[1] + 1, sizes[1]), 0, 1)
    inside = pieces.shape[2:]
    pieces = pieces.reshape(-1, *inside)
    pieces = lax.all_to_all(pieces, axis, split_axis=0, concat_axis=0, tiled=True)
    pieces = laid_out(pieces.reshape(*sizes, *inside), concats[0] + 1)
    return laid_out(pieces, concats[1])


def rms_scale(values, gain_vec):
    mean_sq = jnp.mean(values * values, axis=-1, keepdims=True)
    return values * lax.rsqrt(mean_sq + epsilon) * gain_vec


def expert_rows(inputs, gate_weight, up_weight, down_weight):
    gate_act = jnp.dot(inputs, gate_weight, preferred_element_type=jnp.float32)
    up_act = jnp.dot(inputs, up_weight, preferred_element_type=jnp.float32)
    hidden = (jax.nn.silu(gate_act) * up_act).astype(jnp.bfloat16)
    return jnp.dot(hidden, down_weight, preferred_element_type=jnp.float32).astype(jnp.bfloat16)


def local(
    tokens,
    attn_gain,
    w_query,
    w_key,
    w_value,
    w_gate,
    head_gain,
    w_out,
    moe_gain,
    w_router,
    expert_picks,
    exp_gate,
    exp_up,
    exp_down,
):
    gathered = gather_directly(tokens, "head", 2)
    seq_count, length, model_width = gathered.shape
    flat_tokens = gathered.reshape(seq_count * length, model_width)
    normed = rms_scale(flat_tokens.astype(jnp.float32), attn_gain).astype(jnp.bfloat16)
    head_width = w_query.shape[1]
    heads_here = head_width // DH
    block_count = length // BLOCK

    def project(weight):
        return jnp.dot(normed, weight, preferred_element_type=jnp.float32)

    block_shape = (seq_count, block_count, BLOCK, heads_here, DH)
    query_blocks = jax.nn.silu(project(w_query)).astype(jnp.bfloat16).reshape(block_shape)
    key_blocks = jax.nn.silu(project(w_key)).astype(jnp.bfloat16).reshape(block_shape)
    value_blocks = jax.nn.silu(project(w_value)).astype(jnp.bfloat16).reshape(block_shape)
    gate_out = jax.nn.sigmoid(project(w_gate))
    causal = jnp.arange(BLOCK)[:, None] >= jnp.arange(BLOCK)[None, :]
    scores = jnp.einsum(
        "snihd,snjhd->snhij", query_blocks, key_blocks, preferred_element_type=jnp.float32
    )
    scores = jnp.where(causal, scores, 0.0).astype(jnp.bfloat16)
    inner_part = jnp.einsum(
        "snhij,snjhd->snihd", scores, value_blocks, preferred_element_type=jnp.float32
    )
    block_states = jnp.einsum(
        "snjhd,snjhe->snhde", key_blocks, value_blocks, preferred_element_type=jnp.float32
    )
    local_total = jnp.sum(block_states, axis=1)
    own_index = lax.axis_index("seq")
    shards = gather_directly(local_total[None].astype(jnp.bfloat16), "seq", 0).astype(jnp.float32)
    owners = jnp.arange(shards.shape[0], dtype=jnp.int32)
    keep_mask = (owners < own_index)[:, None, None, None, None]
    carried = jnp.zeros_like(local_total) + jnp.sum(jnp.where(keep_mask, shards, 0.0), axis=0)
    within = jnp.cumsum(block_states, axis=1) - block_states
    prefix = (carried[:, None] + within).astype(jnp.bfloat16)
    outer_part = jnp.einsum(
        "snihd,snhde->snihe", query_blocks, prefix, preferred_element_type=jnp.float32
    )
    mixed = (inner_part + outer_part).reshape(seq_count * length, heads_here, DH)
    normed_heads = rms_scale(mixed, head_gain.reshape(heads_here, DH))
    gated_out = (normed_heads.reshape(seq_count * length, head_width) * gate_out).astype(
        jnp.bfloat16
    )
    row_count = expert_picks.shape[1]
    attn_rows = summed_on_arrival(
        jnp.dot(gated_out, w_out, preferred_element_type=jnp.float32).astype(jnp.bfloat16),
        "head",
        0,
    )
    first_row = lax.axis_index("head") * row_count
    residual = (
        lax.dynamic_slice_in_dim(flat_tokens, first_row, row_count, 0).astype(jnp.float32)
        + attn_rows
    )
    moe_in = rms_scale(residual, moe_gain).astype(jnp.bfloat16)
    logits = jnp.dot(moe_in, w_router, preferred_element_type=jnp.float32)
    chosen = expert_picks[0]
    experts = w_router.shape[1]
    pick_count = chosen.shape[1]
    pick_match = chosen[:, :, None] == jnp.arange(experts, dtype=jnp.int32)[None, None, :]
    picked = jnp.sum(jnp.where(pick_match, logits[:, None, :], 0.0), axis=2)
    pick_scores = jax.nn.sigmoid(picked)
    weights = pick_scores / jnp.sum(pick_scores, axis=1, keepdims=True)
    one_hot = pick_match.reshape(row_count * pick_count, experts).astype(jnp.int32)
    before = jnp.cumsum(one_hot, axis=0) - one_hot
    slot_index = jnp.sum(before * one_hot, axis=1)
    capacity = 3 * row_count * pick_count // (2 * experts)
    position = chosen.reshape(-1) * capacity + slot_index
    sources = jnp.broadcast_to(moe_in[:, None, :], (row_count, pick_count, model_width)).reshape(
        row_count * pick_count, model_width
    )
    outgoing = jnp.zeros((experts * capacity, model_width), jnp.bfloat16).at[position].set(sources)
    gate_weight = exp_gate[0]
    up_weight = exp_up[0]
    down_weight = exp_down[0]
    seq_size = lax.axis_size("seq")
    head_size = lax.axis_size("head")
    arrived = exchange_both(
        outgoing.reshape(seq_size, head_size, capacity, model_width),
        ("seq", "head"),
        ("seq", "head"),
        (0, 1),
        (0, 1),
    )
    result = expert_rows(arrived.reshape(-1, model_width), gate_weight, up_weight, down_weight)
    result = result.reshape(seq_size, head_size, capacity, model_width)
    returned = exchange_both(result, ("seq", "head"), ("seq", "head"), (0, 1), (0, 1))
    returned = returned.reshape(experts * capacity, model_width)
    gathered_rows = (
        returned[position].astype(jnp.float32).reshape(row_count, pick_count, model_width)
    )
    moe_out = jnp.sum(weights[:, :, None] * gathered_rows, axis=1)
    return (residual + moe_out)[None]


def solution(mesh):
    placed = (
        P(None, "seq", "head"),
        P(),
        P(None, "head"),
        P(None, "head"),
        P(None, "head"),
        P(None, "head"),
        P("head"),
        P("head", None),
        P(),
        P(),
        P("seq", "head", None),
        P(("seq", "head"), None, None),
        P(("seq", "head"), None, None),
        P(("seq", "head"), None, None),
    )
    return jax.shard_map(
        local, mesh=mesh, in_specs=placed, out_specs=P("seq", "head", None), check_vma=False
    )
```

profile of v0, /device:TPU:1, one launch (start us, length us, event | category | flops | bytes accessed | tf_op | source)
XLA Modules:
  0.0 243.0 jit_solution(13623250762316081543)
XLA Ops:
  0.0 0.0 copy-start
  0.0 1.5 broadcast_in_dim.42
  1.5 34.7 %all_to_all.25 = bf16[16,2,256,128]{3,2,1,0:T(8,128)(2,1)S(1)} all-to-all(bf16[16,2,256,128]{3,2,1,0:T(8,128)(2,1)S(1)} %broadcast_in_dim.42), channel_id=1, replica_groups=mesh['seq'=8,'head'=16] {'head'}, dimensions={0} | all-to-all | bytes 4194304 | tf_op jit(solution)/shard_map/all_to_all | solution.py:21
  36.3 1.4 copy.86
  37.6 0.0 copy-start.1
  37.6 0.0 copy-start.4
  37.7 0.5 multiply_reduce_fusion
  38.2 0.2 copy-done.4
  38.4 0.6 multiply_convert_fusion
  39.0 0.0 copy-done.1
  39.0 0.0 copy-start.2
  39.0 1.3 copy-done.2
  40.3 1.4 multiply_convert_fusion.1
  41.7 1.0 reshape.200
  42.7 0.9 copy.90
  43.6 2.6 %multiply_convert_fusion.3 = bf16[512,256]{1,0:T(8,128)(2,1)S(1)} fusion(bf16[512,2048]{1,0:T(8,128)(2,1)} %copy-done.2, bf16[2048,256]{1,0:T(8,128)(2,1)} %param.18), kind=kOutput, calls=%fused_computation.45 | convolution fusion | flops 537526272 | bytes 3407872 | tf_op jit(solution)/shard_map/dot_general | solution.py:87
  46.2 0.8 reshape.198
  47.0 1.2 fusion.57
  48.2 1.3 broadcast_in_dim.70
  49.5 7.3 %all-to-all-start.1 = ((bf16[8,1,2,2,128,128]{5,4,3,2,1,0:T(8,128)(2,1)}), bf16[8,1,2,2,128,128]{5,4,3,2,1,0:T(8,128)(2,1)}, u32[]{:S(2)}, u32[]{:S(2)}) async-start(bf16[8,1,2,2,128,128]{5,4,3,2,1,0:T(8,128)(2,1)} %broadcast_in_dim.70), calls=%async_computation.1 | async-start | bytes 2097152 | tf_op jit(solution)/shard_map/all_to_all | solution.py:21
  56.8 3.3 %multiply_convert_fusion.2 = bf16[512,256]{1,0:T(8,128)(2,1)} fusion(bf16[512,2048]{1,0:T(8,128)(2,1)} %copy-done.2, bf16[2048,256]{1,0:T(8,128)(2,1)} %param.16), kind=kOutput, calls=%fused_computation.44 | convolution fusion | flops 537526272 | bytes 3407872 | tf_op jit(solution)/shard_map/dot_general | solution.py:87
  60.1 1.7 reshape.199
  61.8 10.2 %all-to-all-done.1 = bf16[8,1,2,2,128,128]{5,4,3,2,1,0:T(8,128)(2,1)} async-done(((bf16[8,1,2,2,128,128]{5,4,3,2,1,0:T(8,128)(2,1)}), bf16[8,1,2,2,128,128]{5,4,3,2,1,0:T(8,128)(2,1)}, u32[]{:S(2)}, u32[]{:S(2)}) %all-to-all-start.1) | async-done | bytes 1048608 | tf_op jit(solution)/shard_map/all_to_all | solution.py:21
  72.0 1.5 fusion.10
  73.5 2.0 fusion.45
  75.5 2.6 %multiply_reduce_fusion.1 = (f32[2,256,2]{1,2,0:T(2,128)S(1)}, f32[2,1,256,2,128]{2,4,3,0,1:T(8,128)}) fusion(f32[2,2,128,256]{3,2,1,0:T(8,128)} %fusion.45, bf16[2,256,2,128]{1,3,2,0:T(8,128)(2,1)} %copy.90, pred[256,256]{1,0:T(8,128)(4,1)S(1)} %iota_compare_fusion, bf16[2,256,2,128]{3,2,1,0:T(2,128)(2,1)} %reshape.199, bf16[2,256,2,128]{3,2,1,0:T(2,128)(2,1)} %reshape.198), kind=kOutput, calls=%fused_computation.41 | convolution fusion | flops 135134208 | bytes 1904640 | tf_op jit(solution)/shard_map/snhij,snjhd->snihd/dot_general | solution.py:99
  78.1 0.1 copy.95
  78.2 2.1 copy.94
  80.3 1.4 mul.123
  81.7 0.0 copy-done.8
  81.7 6.1 %convolution_convert_fusion = bf16[512,2048]{1,0:T(8,128)(2,1)} fusion(bf16[256,2048]{1,0:T(8,128)(2,1)} %param.21, bf16[512,2048]{1,0:T(8,128)(2,1)} %copy-done.2, bf16[2048,256]{1,0:T(8,128)(2,1)} %param.19, f32[64,8,2,128]{3,2,1,0:T(2,128)} %bitcast.124, f32[64,8,2,128]{3,2,1,0:T(2,128)} %bitcast.125, f32[256]{0:T(256)S(1)} %copy-done.8), kind=kOutput, calls=%fused_computation.11 | convolution fusion | flops 1075707904 | bytes 7341056 | tf_op jit(solution)/shard_map/dot_general | solution.py:123
  87.9 4.7 %all-to-all-start.2 = ((bf16[16,32,2048]{2,1,0:T(8,128)(2,1)}), bf16[16,32,2048]{2,1,0:T(8,128)(2,1)}, u32[]{:S(2)}, u32[]{:S(2)}) async-start(bf16[16,32,2048]{2,1,0:T(8,128)(2,1)} %bitcast.122), calls=%async_computation.2 | async-start | bytes 4194304 | tf_op jit(solution)/shard_map/all_to_all | solution.py:35
  92.6 0.1 copy.100
  92.7 0.1 eq.42
  92.8 0.1 eq.38
  92.9 0.1 copy.102
  93.0 0.2 fusion.49
  93.3 0.1 copy.99
  93.4 0.1 mul.137
  93.5 0.2 fusion.51
  93.7 3.4 %copy.137 = bf16[64,8,16,128]{3,1,2,0:T(8,128)(2,1)} copy(bf16[64,8,16,128]{3,2,1,0:T(8,128)(2,1)} %bitcast.115) | data formatting | bytes 4194304
  97.1 26.4 %all-to-all-done.2 = bf16[16,32,2048]{2,1,0:T(8,128)(2,1)} async-done(((bf16[16,32,2048]{2,1,0:T(8,128)(2,1)}), bf16[16,32,2048]{2,1,0:T(8,128)(2,1)}, u32[]{:S(2)}, u32[]{:S(2)}) %all-to-all-start.2) | async-done | bytes 2097184 | tf_op jit(solution)/shard_map/all_to_all | solution.py:35
  123.5 2.0 convert_reduce_fusion
  125.5 1.1 multiply_reduce_fusion.2
  126.6 1.0 multiply_convert_fusion.4
  127.6 3.5 %scatter_custom_fusion = bf16[384,2048]{1,0:T(8,128)(2,1)} fusion(s32[256]{0:T(256)S(1)} %bitcast.132, bf16[]{:T(256)} %constant.49.clone.1, bf16[32,2048]{1,0:T(8,128)(2,1)S(1)} %multiply_convert_fusion.4), kind=kCustom, calls=%fused_computation.31 | custom fusion | bytes 1703938 | tf_op jit(solution)/shard_map/scatter | solution.py:149
  131.0 5.1 %reshape_transpose_transpose_reshape_reshape_reshape.6 = bf16[128,1,1,3,2048]{4,3,0,2,1:T(4,128)(2,1)} reshape(bf16[384,2048]{1,0:T(8,128)(2,1)} %scatter_custom_fusion) | data formatting | bytes 3145728 | tf_op jit(solution)/shard_map/reshape;transpose;transpose;reshape;reshape;reshape | solution.py:44
  136.2 35.9 %all_to_all.26 = bf16[128,1,1,3,2048]{4,3,2,1,0:T(4,128)(2,1)} all-to-all(bf16[128,1,1,3,2048]{4,3,2,1,0:T(4,128)(2,1)} %bitcast.117), channel_id=1, replica_groups=mesh['seq'=8,'head'=16] {'seq','head'}, dimensions={0} | all-to-all | bytes 3145728 | tf_op jit(solution)/shard_map/all_to_all | solution.py:45
  172.1 5.0 %reshape_reshape.10 = bf16[384,2048]{1,0:T(8,128)(2,1)} reshape(bf16[8,16,1,3,2048]{4,3,1,0,2:T(4,128)(2,1)} %bitcast.118) | data formatting | bytes 3145728 | tf_op jit(solution)/shard_map/reshape;reshape | solution.py:162
  177.2 4.8 %fusion.4 = f32[384,768]{1,0:T(8,128)} fusion(bf16[384,2048]{1,0:T(8,128)(2,1)} %reshape_reshape.10, bf16[1,2048,768]{2,1,0:T(8,128)(2,1)} %param.25), kind=kOutput, calls=%fused_computation.9 | convolution fusion | flops 1207959552 | bytes 5898240 | tf_op jit(solution)/shard_map/dot_general | solution.py:56
  181.9 6.9 %fusion.6 = bf16[384,2048]{1,0:T(8,128)(2,1)} fusion(bf16[1,768,2048]{2,1,0:T(8,128)(2,1)S(1)} %copy-done, bf16[384,2048]{1,0:T(8,128)(2,1)} %reshape_reshape.10, bf16[1,2048,768]{2,1,0:T(8,128)(2,1)} %param.26, f32[384,768]{1,0:T(8,128)} %fusion.4), kind=kOutput, calls=%fused_computation.12 | convolution fusion | flops 2418475008 | bytes 10616832 | tf_op jit(solution)/shard_map/dot_general | solution.py:59
  188.8 5.2 %reshape_transpose_transpose_reshape_reshape_reshape.7 = bf16[128,1,1,3,2048]{4,3,0,2,1:T(4,128)(2,1)} reshape(bf16[384,2048]{1,0:T(8,128)(2,1)} %fusion.6) | data formatting | bytes 3145728 | tf_op jit(solution)/shard_map/reshape;transpose;transpose;reshape;reshape;reshape | solution.py:44
  193.9 5.6 %all-to-all-start.4 = ((bf16[128,1,1,3,2048]{4,3,2,1,0:T(4,128)(2,1)}), bf16[128,1,1,3,2048]{4,3,2,1,0:T(4,128)(2,1)}, u32[]{:S(2)}, u32[]{:S(2)}) async-start(bf16[128,1,1,3,2048]{4,3,2,1,0:T(4,128)(2,1)} %bitcast.116), calls=%async_computation.4 | async-start | bytes 4194304 | tf_op jit(solution)/shard_map/all_to_all | solution.py:45
  199.5 0.8 copy.96
  200.3 1.2 pad_clamp_fusion
  201.5 1.2 fusion.60
  202.7 0.2 select_reduce_fusion
  202.9 0.1 copy.97
  203.0 0.1 copy.98
  203.1 25.9 %all-to-all-done.4 = bf16[128,1,1,3,2048]{4,3,2,1,0:T(4,128)(2,1)} async-done(((bf16[128,1,1,3,2048]{4,3,2,1,0:T(4,128)(2,1)}), bf16[128,1,1,3,2048]{4,3,2,1,0:T(4,128)(2,1)}, u32[]{:S(2)}, u32[]{:S(2)}) %all-to-all-start.4) | async-done | bytes 1572896 | tf_op jit(solution)/shard_map/all_to_all | solution.py:45
  229.0 5.0 %reshape_reshape.11 = bf16[384,2048]{1,0:T(8,128)(2,1)} reshape(bf16[8,16,1,3,2048]{4,3,1,0,2:T(4,128)(2,1)} %bitcast.26) | data formatting | bytes 3145728 | tf_op jit(solution)/shard_map/reshape;reshape | solution.py:165
  234.0 5.1 %gather_fusion = bf16[256,2048]{1,0:T(8,128)(2,1)} fusion(bf16[384,2048]{1,0:T(8,128)(2,1)} %reshape_reshape.11, s32[1024]{0:T(1024)} %pad_clamp_fusion), kind=kCustom, calls=%fused_computation | custom fusion | bytes 2098176 | tf_op jit(solution)/shard_map/gather | solution.py:167
  239.1 2.2 fusion.9
  241.3 1.7 add_bitcast_fusion
  (26 shorter events, 0.2 us)
Async XLA Ops:
  0.0 181.9 %copy-start = (bf16[1,768,2048]{2,1,0:T(8,128)(2,1)S(1)}, bf16[1,768,2048]{2,1,0:T(8,128)(2,1)}, u32[]{:S(2)}) copy-start(bf16[1,768,2048]{2,1,0:T(8,128)(2,1)} %param.27) | copy-start | bytes 9437188
  37.6 1.4 copy-start.1
  37.6 0.7 copy-start.4
  38.4 1.9 copy-start.7
  39.0 1.3 copy-start.2
  49.5 22.5 %all-to-all-start.1 = ((bf16[8,1,2,2,128,128]{5,4,3,2,1,0:T(8,128)(2,1)}), bf16[8,1,2,2,128,128]{5,4,3,2,1,0:T(8,128)(2,1)}, u32[]{:S(2)}, u32[]{:S(2)}) async-start(bf16[8,1,2,2,128,128]{5,4,3,2,1,0:T(8,128)(2,1)} %broadcast_in_dim.70), calls=%async_computation.1 | async-start | bytes 2097152 | tf_op jit(solution)/shard_map/all_to_all | solution.py:21
  75.5 6.2 %copy-start.8 = (f32[256]{0:T(256)S(1)}, f32[256]{0:T(256)}, u32[]{:S(2)}) copy-start(f32[256]{0:T(256)} %param.20) | copy-start | bytes 3076
  87.8 4.8 %copy-start.3 = (s32[1,32,8]{1,2,0:T(8,128)S(1)}, s32[1,32,8]{1,2,0:T(8,128)}, u32[]{:S(2)}) copy-start(s32[1,32,8]{1,2,0:T(8,128)} %param.24) | copy-start | bytes 3076
  87.9 35.6 %all-to-all-start.2 = ((bf16[16,32,2048]{2,1,0:T(8,128)(2,1)}), bf16[16,32,2048]{2,1,0:T(8,128)(2,1)}, u32[]{:S(2)}, u32[]{:S(2)}) async-start(bf16[16,32,2048]{2,1,0:T(8,128)(2,1)} %bitcast.122), calls=%async_computation.2 | async-start | bytes 4194304 | tf_op jit(solution)/shard_map/all_to_all | solution.py:35
  93.7 33.9 %copy-start.6 = (s32[256,1]{0,1:T(1,128)}, s32[256,1]{0,1:T(1,128)S(1)}, u32[]{:S(2)}) copy-start(s32[256,1]{0,1:T(1,128)S(1)} %compare_select_fusion) | copy-start | bytes 3076
  97.1 29.4 %copy-start.5 = (f32[2048]{0:T(1024)S(1)}, f32[2048]{0:T(1024)}, u32[]{:S(2)}) copy-start(f32[2048]{0:T(1024)} %param.22) | copy-start | bytes 24580
  193.9 35.1 %all-to-all-start.4 = ((bf16[128,1,1,3,2048]{4,3,2,1,0:T(4,128)(2,1)}), bf16[128,1,1,3,2048]{4,3,2,1,0:T(4,128)(2,1)}, u32[]{:S(2)}, u32[]{:S(2)}) async-start(bf16[128,1,1,3,2048]{4,3,2,1,0:T(4,128)(2,1)} %bitcast.116), calls=%async_computation.4 | async-start | bytes 4194304 | tf_op jit(solution)/shard_map/all_to_all | solution.py:45
where the time goes:
time: 244 us; the launch traced here: 243 us
  blocking collectives  70.7 us (29%)
  waiting for transfers between devices  62.4 us (26%)
  local copies, waits for them, and re-layouts  47.5 us (19%)
  matrix products  32.1 us (13%)
  starting transfers between devices  17.6 us (7%)
  other arithmetic  12.5 us (5%)
    all_to_all x1, blocking collectives, exchange_both(): lax.all_to_all(pieces, axis, split_axis=0, concat_axis=0, tiled=True)  35.9 us
    all_to_all x1, blocking collectives, from_everyone(): return lax.all_to_all(copies, axis, split_axis=0, concat_axis=0, tiled=True)  34.7 us
    all_to_all x1, waiting for transfers between devices, summed_on_arrival(): lax.all_to_all(pieces, axis, split_axis=0, concat_axis=0, tiled=True)  26.4 us
    all_to_all x1, waiting for transfers between devices, exchange_both(): lax.all_to_all(pieces, axis, split_axis=0, concat_axis=0, tiled=True)  25.9 us
    another operation x2, local copies, waits for them, and re-layouts, exchange_both(): pieces = pieces.reshape(-1, *inside)  10.3 us
    all_to_all x1, waiting for transfers between devices, from_everyone(): return lax.all_to_all(copies, axis, split_axis=0, concat_axis=0, tiled=True)  10.2 us
    dot_general x3, matrix products, project(): return jnp.dot(normed, weight, preferred_element_type=jnp.float32)  7.3 us
    all_to_all x1, starting transfers between devices, from_everyone(): return lax.all_to_all(copies, axis, split_axis=0, concat_axis=0, tiled=True)  7.29 us
  transfers between devices with their start and end apart: 3, of which 3 were waited for; matrix products, arithmetic and copies ran while one was open for 5% of the time, Pallas kernels for 0%

commit v1 on v0

--- a/solution.py
+++ b/solution.py
@@ -1,6 +1,8 @@
 import jax
 import jax.numpy as jnp
 from jax import lax
+from jax.experimental import pallas as pl
+from jax.experimental.pallas import tpu as pltpu
 from jax.sharding import PartitionSpec as P
 
 DH = 128
@@ -36,27 +38,242 @@
     return arrived.astype(jnp.float32).sum(axis=0)
 
 
-def exchange_both(value, axis, axes, splits, concats):
-    sizes = [lax.axis_size(a) for a in axes]
-    pieces = split_up(value, splits[0], sizes[0])
-    pieces = jnp.moveaxis(split_up(pieces, splits[1] + 1, sizes[1]), 0, 1)
-    inside = pieces.shape[2:]
-    pieces = pieces.reshape(-1, *inside)
-    pieces = lax.all_to_all(pieces, axis, split_axis=0, concat_axis=0, tiled=True)
-    pieces = laid_out(pieces.reshape(*sizes, *inside), concats[0] + 1)
-    return laid_out(pieces, concats[1])
-
-
 def rms_scale(values, gain_vec):
     mean_sq = jnp.mean(values * values, axis=-1, keepdims=True)
     return values * lax.rsqrt(mean_sq + epsilon) * gain_vec
 
 
-def expert_rows(inputs, gate_weight, up_weight, down_weight):
-    gate_act = jnp.dot(inputs, gate_weight, preferred_element_type=jnp.float32)
-    up_act = jnp.dot(inputs, up_weight, preferred_element_type=jnp.float32)
-    hidden = (jax.nn.silu(gate_act) * up_act).astype(jnp.bfloat16)
-    return jnp.dot(hidden, down_weight, preferred_element_type=jnp.float32).astype(jnp.bfloat16)
+MESH = pl.DeviceIdType.MESH
+SEQ = 8
+HEAD = 16
+DEVS = SEQ * HEAD
+ROWS = 32
+TOP = 8
+SLOTS = 3
+WIDTH = 2048
+HIDDEN = 768
+TILES = WIDTH // 128
+CHUNK = SLOTS * TILES
+HALF = DEVS // 2
+
+
+def moe_kernel(
+    residual_ref,
+    gain_ref,
+    router_ref,
+    picks_ref,
+    picks_t_ref,
+    gate_hbm,
+    up_hbm,
+    down_hbm,
+    out_ref,
+    gate_w,
+    up_w,
+    down_w,
+    spread,
+    outgoing,
+    arrived,
+    result,
+    returned,
+    rows,
+    weight_sem,
+    out_sem,
+    in_sem,
+    back_out_sem,
+    back_in_sem,
+):
+    my_seq = lax.axis_index("seq")
+    my_head = lax.axis_index("head")
+    me = my_seq * HEAD + my_head
+    loads = [
+        pltpu.make_async_copy(hbm, vmem, weight_sem.at[i])
+        for i, (hbm, vmem) in enumerate(((gate_hbm, gate_w), (up_hbm, up_w), (down_hbm, down_w)))
+    ]
+    for load in loads:
+        load.start()
+
+    barrier = pltpu.get_barrier_semaphore()
+
+    def greet(i, carry):
+        other = lax.rem(me + i, DEVS)
+        pl.semaphore_signal(
+            barrier, inc=1, device_id=(other // HEAD, lax.rem(other, HEAD)), device_id_type=MESH
+        )
+        return carry
+
+    lax.fori_loop(1, DEVS, greet, 0)
+
+    residual = residual_ref[...]
+    moe_in = rms_scale(residual, gain_ref[...]).astype(jnp.bfloat16)
+    logits = jnp.dot(moe_in, router_ref[...], preferred_element_type=jnp.float32)
+    picks = picks_ref[...]
+    picks_t = picks_t_ref[...]
+    lane = lax.broadcasted_iota(jnp.int32, (ROWS, DEVS), 1)
+    line = lax.broadcasted_iota(jnp.int32, (DEVS, ROWS), 0)
+    match = jnp.zeros((ROWS, DEVS), jnp.float32)
+    match_t = jnp.zeros((DEVS, ROWS), jnp.float32)
+    for k in range(TOP):
+        match = match + jnp.where(picks[:, k : k + 1] == lane, 1.0, 0.0)
+        match_t = match_t + jnp.where(picks_t[k : k + 1, :] == line, 1.0, 0.0)
+    row_i = lax.broadcasted_iota(jnp.int32, (ROWS, ROWS), 0)
+    col_i = lax.broadcasted_iota(jnp.int32, (ROWS, ROWS), 1)
+    earlier = jnp.where(col_i < row_i, 1.0, 0.0).astype(jnp.bfloat16)
+    earlier_t = jnp.where(row_i < col_i, 1.0, 0.0).astype(jnp.bfloat16)
+    before = jnp.dot(earlier, match.astype(jnp.bfloat16), preferred_element_type=jnp.float32)
+    before_t = jnp.dot(match_t.astype(jnp.bfloat16), earlier_t, preferred_element_type=jnp.float32)
+    scores = match * jax.nn.sigmoid(logits)
+    weights = scores / jnp.sum(scores, axis=1, keepdims=True)
+    select = jnp.concatenate(
+        [jnp.where(before_t == float(c), match_t, 0.0) for c in range(SLOTS)], axis=0
+    ).astype(jnp.bfloat16)
+    for j in range(0, TILES, 2):
+        picked = jnp.dot(
+            select, moe_in[:, j * 128 : (j + 2) * 128], preferred_element_type=jnp.float32
+        )
+        for c in range(SLOTS):
+            for half in range(2):
+                spread[pl.ds(c * TILES + j + half, DEVS, CHUNK), :] = picked[
+                    c * DEVS : (c + 1) * DEVS, half * 128 : (half + 1) * 128
+                ]
+    pl.semaphore_wait(barrier, DEVS - 1)
+
+    for o in range(SEQ):
+        to_seq = lax.rem(my_seq + o, SEQ)
+        part = pl.multiple_of(to_seq * (HEAD * CHUNK), HEAD * CHUNK)
+        outgoing[pl.ds(to_seq * HEAD, HEAD)] = (
+            spread[pl.ds(part, HEAD * CHUNK), :].astype(jnp.bfloat16).reshape(HEAD, CHUNK, 128)
+        )
+
+        def send(i, carry):
+            to_head = lax.rem(my_head + i, HEAD)
+            pltpu.make_async_remote_copy(
+                src_ref=outgoing.at[to_seq * HEAD + to_head],
+                dst_ref=arrived.at[o * HEAD + my_head],
+                send_sem=out_sem,
+                recv_sem=in_sem.at[o],
+                device_id=(to_seq, to_head),
+                device_id_type=MESH,
+            ).start()
+            return carry
+
+        if o == 0:
+            pltpu.make_async_copy(
+                outgoing.at[me], arrived.at[my_head], in_sem.at[0]
+            ).start()
+        lax.fori_loop(1 if o == 0 else 0, HEAD, send, 0)
+
+    for load in loads:
+        load.wait()
+    part_rows = HALF * SLOTS
+    for part in range(2):
+        for o in range(part * SEQ // 2, (part + 1) * SEQ // 2):
+            group = arrived.at[pl.ds(o * HEAD, HEAD)]
+            pltpu.make_async_copy(group, group, in_sem.at[o]).wait()
+        for q in range(4):
+            block = arrived[pl.ds(part * HALF + q * HEAD, HEAD)]
+            spread[pl.ds(q * HEAD * CHUNK, HEAD * CHUNK), :] = block.astype(jnp.float32).reshape(
+                HEAD * CHUNK, 128
+            )
+        for j in range(TILES):
+            rows[0:part_rows, j * 128 : (j + 1) * 128] = spread[
+                pl.ds(j, part_rows, TILES), :
+            ].astype(jnp.bfloat16)
+        inputs = rows[0:part_rows, :]
+        gate_act = jnp.dot(inputs, gate_w[...], preferred_element_type=jnp.float32)
+        up_act = jnp.dot(inputs, up_w[...], preferred_element_type=jnp.float32)
+        hidden = (jax.nn.silu(gate_act) * up_act).astype(jnp.bfloat16)
+        for j in range(0, TILES, 2):
+            produced = jnp.dot(
+                hidden, down_w[:, j * 128 : (j + 2) * 128], preferred_element_type=jnp.float32
+            )
+            for half in range(2):
+                spread[pl.ds(j + half, part_rows, TILES), :] = produced[
+                    :, half * 128 : (half + 1) * 128
+                ]
+        for o in range(part * SEQ // 2, (part + 1) * SEQ // 2):
+            q = o - part * SEQ // 2
+            result[pl.ds(o * HEAD, HEAD)] = (
+                spread[pl.ds(q * HEAD * CHUNK, HEAD * CHUNK), :]
+                .astype(jnp.bfloat16)
+                .reshape(HEAD, CHUNK, 128)
+            )
+            to_seq = lax.rem(my_seq + SEQ - o, SEQ)
+
+            def send_back(i, carry):
+                to_head = lax.rem(my_head + i, HEAD)
+                pltpu.make_async_remote_copy(
+                    src_ref=result.at[o * HEAD + to_head],
+                    dst_ref=returned.at[me],
+                    send_sem=back_out_sem,
+                    recv_sem=back_in_sem,
+                    device_id=(to_seq, to_head),
+                    device_id_type=MESH,
+                ).start()
+                return carry
+
+            if o == 0:
+                pltpu.make_async_copy(
+                    result.at[my_head], returned.at[me], back_in_sem
+                ).start()
+            lax.fori_loop(1 if o == 0 else 0, HEAD, send_back, 0)
+
+    pltpu.make_async_copy(returned, returned, back_in_sem).wait()
+    for q in range(SEQ):
+        spread[pl.ds(q * HEAD * CHUNK, HEAD * CHUNK), :] = (
+            returned[pl.ds(q * HEAD, HEAD)].astype(jnp.float32).reshape(HEAD * CHUNK, 128)
+        )
+    for c in range(SLOTS):
+        for j in range(TILES):
+            rows[c * DEVS : (c + 1) * DEVS, j * 128 : (j + 1) * 128] = spread[
+                pl.ds(c * TILES + j, DEVS, CHUNK), :
+            ].astype(jnp.bfloat16)
+    spread_weights = jnp.concatenate(
+        [jnp.where(before == float(c), weights, 0.0) for c in range(SLOTS)], axis=1
+    )
+    high = spread_weights.astype(jnp.bfloat16)
+    low = (spread_weights - high.astype(jnp.float32)).astype(jnp.bfloat16)
+    both = jnp.dot(
+        jnp.concatenate([high, low], axis=0), rows[...], preferred_element_type=jnp.float32
+    )
+    out_ref[...] = both[:ROWS] + both[ROWS:]
+    sent = outgoing.at[pl.ds(0, DEVS - 1)]
+    pltpu.make_async_copy(sent, sent, out_sem).wait()
+    sent_back = result.at[pl.ds(0, DEVS - 1)]
+    pltpu.make_async_copy(sent_back, sent_back, back_out_sem).wait()
+
+
+def moe(residual, gain, router, picks, gate_weight, up_weight, down_weight):
+    vmem = pl.BlockSpec(memory_space=pltpu.VMEM)
+    anywhere = pl.BlockSpec(memory_space=pl.ANY)
+    chunks = pltpu.VMEM((DEVS, CHUNK, 128), jnp.bfloat16)
+    return pl.pallas_call(
+        moe_kernel,
+        out_shape=jax.ShapeDtypeStruct((ROWS, WIDTH), jnp.float32),
+        in_specs=[vmem] * 5 + [anywhere] * 3,
+        out_specs=vmem,
+        scratch_shapes=[
+            pltpu.VMEM((WIDTH, HIDDEN), jnp.bfloat16),
+            pltpu.VMEM((WIDTH, HIDDEN), jnp.bfloat16),
+            pltpu.VMEM((HIDDEN, WIDTH), jnp.bfloat16),
+            pltpu.VMEM((DEVS * CHUNK, 128), jnp.float32),
+            chunks,
+            chunks,
+            chunks,
+            chunks,
+            pltpu.VMEM((DEVS * SLOTS, WIDTH), jnp.bfloat16),
+            pltpu.SemaphoreType.DMA((3,)),
+            pltpu.SemaphoreType.DMA,
+            pltpu.SemaphoreType.DMA((SEQ,)),
+            pltpu.SemaphoreType.DMA,
+            pltpu.SemaphoreType.DMA,
+        ],
+        compiler_params=pltpu.CompilerParams(
+            collective_id=1, has_side_effects=True, vmem_limit_bytes=48 * 1024 * 1024
+        ),
+        cost_estimate=pl.CostEstimate(
+            flops=6 * DEVS * SLOTS * WIDTH * HIDDEN, bytes_accessed=10 << 20, transcendentals=0
+        ),
+    )(residual, gain, router, picks, picks.T, gate_weight, up_weight, down_weight)
 
 
 def local(
@@ -129,44 +346,15 @@
         lax.dynamic_slice_in_dim(flat_tokens, first_row, row_count, 0).astype(jnp.float32)
         + attn_rows
     )
-    moe_in = rms_scale(residual, moe_gain).astype(jnp.bfloat16)
-    logits = jnp.dot(moe_in, w_router, preferred_element_type=jnp.float32)
-    chosen = expert_picks[0]
-    experts = w_router.shape[1]
-    pick_count = chosen.shape[1]
-    pick_match = chosen[:, :, None] == jnp.arange(experts, dtype=jnp.int32)[None, None, :]
-    picked = jnp.sum(jnp.where(pick_match, logits[:, None, :], 0.0), axis=2)
-    pick_scores = jax.nn.sigmoid(picked)
-    weights = pick_scores / jnp.sum(pick_scores, axis=1, keepdims=True)
-    one_hot = pick_match.reshape(row_count * pick_count, experts).astype(jnp.int32)
-    before = jnp.cumsum(one_hot, axis=0) - one_hot
-    slot_index = jnp.sum(before * one_hot, axis=1)
-    capacity = 3 * row_count * pick_count // (2 * experts)
-    position = chosen.reshape(-1) * capacity + slot_index
-    sources = jnp.broadcast_to(moe_in[:, None, :], (row_count, pick_count, model_width)).reshape(
-        row_count * pick_count, model_width
-    )
-    outgoing = jnp.zeros((experts * capacity, model_width), jnp.bfloat16).at[position].set(sources)
-    gate_weight = exp_gate[0]
-    up_weight = exp_up[0]
-    down_weight = exp_down[0]
-    seq_size = lax.axis_size("seq")
-    head_size = lax.axis_size("head")
-    arrived = exchange_both(
-        outgoing.reshape(seq_size, head_size, capacity, model_width),
-        ("seq", "head"),
-        ("seq", "head"),
-        (0, 1),
-        (0, 1),
-    )
-    result = expert_rows(arrived.reshape(-1, model_width), gate_weight, up_weight, down_weight)
-    result = result.reshape(seq_size, head_size, capacity, model_width)
-    returned = exchange_both(result, ("seq", "head"), ("seq", "head"), (0, 1), (0, 1))
-    returned = returned.reshape(experts * capacity, model_width)
-    gathered_rows = (
-        returned[position].astype(jnp.float32).reshape(row_count, pick_count, model_width)
-    )
-    moe_out = jnp.sum(weights[:, :, None] * gathered_rows, axis=1)
+    moe_out = moe(
+        residual,
+        moe_gain[None],
+        w_router,
+        expert_picks[0],
+        exp_gate[0],
+        exp_up[0],
+        exp_down[0],
+    )
     return (residual + moe_out)[None]
 
 

time: 244 us -> 189 us (0.77)
  Pallas kernels: 0 us -> 57.4 us
  blocking collectives: 70.7 us -> 34.7 us
  local copies, waits for them, and re-layouts: 47.5 us -> 17.4 us
  waiting for transfers between devices: 62.4 us -> 39.1 us
  matrix products: 32.1 us -> 18.9 us
  other arithmetic: 12.5 us -> 6.35 us
  starting transfers between devices: 17.6 us -> 12 us
    pallas_call x0 -> x1, Pallas kernels: none -> 57.4 us  [moe(): pl.pallas_call(moe_kernel, out_shape=jax.ShapeDtypeStruct((ROWS, WIDTH),...]
    all_to_all x1 -> x0, blocking collectives: 35.9 us -> none  [exchange_both(): lax.all_to_all(pieces, axis, split_axis=0, concat_axis=0, tiled=True)]
    all_to_all x1 -> x0, waiting for transfers between devices: 25.9 us -> none  [exchange_both(): lax.all_to_all(pieces, axis, split_axis=0, concat_axis=0, tiled=True)]
    another operation x11 -> x3, local copies, waits for them, and re-layouts: 24.8 us -> 2.64 us  [the longest x2 10.3 us: exchange_both(): pieces = pieces.reshape(-1, *inside)]
    dot_general x3 -> x0, matrix products: 12.9 us -> none  [the longest x1 6.87 us: expert_rows(): jnp.dot(hidden, down_weight, preferred_element_type=jnp.float32)]
    all_to_all x1 -> x0, starting transfers between devices: 5.57 us -> none  [exchange_both(): lax.all_to_all(pieces, axis, split_axis=0, concat_axis=0, tiled=True)]
    gather x1 -> x0, local copies, waits for them, and re-layouts: 5.1 us -> none  [local(): returned[position].astype(jnp.float32)]
    scatter x1 -> x0, local copies, waits for them, and re-layouts: 3.45 us -> none  [local(): jnp.zeros((experts * capacity, model_width), jnp.bfloat16).at[position]]
  transfers between devices with their start and end apart: 3 -> 2, of which waited for: 3 -> 2; matrix products, arithmetic and copies ran while one was open for 5% -> 4% of each run, Pallas kernels for 0% -> 0%
where the time goes in v1:
time: 189 us; the launch traced here: 186 us
  Pallas kernels  57.4 us (30%)
  waiting for transfers between devices  39.1 us (21%)
  blocking collectives  34.7 us (18%)
  matrix products  18.9 us (10%)
  local copies, waits for them, and re-layouts  17.4 us (9%)
  starting transfers between devices  12 us (6%)
  other arithmetic  6.35 us (3%)
    pallas_call x1, Pallas kernels, moe(): pl.pallas_call(moe_kernel, out_shape=jax.ShapeDtypeStruct((ROWS, WIDTH),...  57.4 us
    all_to_all x1, blocking collectives, from_everyone(): return lax.all_to_all(copies, axis, split_axis=0, concat_axis=0, tiled=True)  34.7 us
    all_to_all x1, waiting for transfers between devices, summed_on_arrival(): lax.all_to_all(pieces, axis, split_axis=0, concat_axis=0, tiled=True)  28.9 us
    all_to_all x1, waiting for transfers between devices, from_everyone(): return lax.all_to_all(copies, axis, split_axis=0, concat_axis=0, tiled=True)  10.2 us
    dot_general x3, matrix products, project(): return jnp.dot(normed, weight, preferred_element_type=jnp.float32)  7.3 us
    all_to_all x1, starting transfers between devices, from_everyone(): return lax.all_to_all(copies, axis, split_axis=0, concat_axis=0, tiled=True)  7.29 us
    dot_general x1, matrix products, local(): jnp.dot(gated_out, w_out, preferred_element_type=jnp.float32)  5.78 us
    unnamed x20, local copies, waits for them, and re-layouts  5.27 us
  transfers between devices with their start and end apart: 2, of which 2 were waited for; matrix products, arithmetic and copies ran while one was open for 4% of the time, Pallas kernels for 0%

profile of v1, /device:TPU:1, one launch (start us, length us, event | category | flops | bytes accessed | tf_op | source)
XLA Modules:
  0.0 186.0 jit_solution(17428884327288044063)
XLA Ops:
  0.0 0.0 copy-start
  0.0 1.5 broadcast_in_dim.40
  1.5 34.7 %all_to_all.15 = bf16[16,2,256,128]{3,2,1,0:T(8,128)(2,1)S(1)} all-to-all(bf16[16,2,256,128]{3,2,1,0:T(8,128)(2,1)S(1)} %broadcast_in_dim.40), channel_id=1, replica_groups=mesh['seq'=8,'head'=16] {'head'}, dimensions={0} | all-to-all | bytes 4194304 | tf_op jit(solution)/shard_map/all_to_all | solution.py:23
  36.2 1.4 copy.30
  37.6 0.0 copy-start.6
  37.6 0.5 multiply_reduce_fusion
  38.1 0.2 copy-done.6
  38.3 0.0 copy-start.7
  38.3 0.6 multiply_convert_fusion
  38.9 0.0 copy-start.5
  38.9 1.3 copy-done.5
  40.2 0.0 copy-done.7
  40.2 1.4 multiply_convert_fusion.1
  41.7 1.0 reshape.102
  42.7 0.8 copy.34
  43.5 2.6 %multiply_convert_fusion.3 = bf16[512,256]{1,0:T(8,128)(2,1)S(1)} fusion(bf16[512,2048]{1,0:T(8,128)(2,1)} %copy-done.5, bf16[2048,256]{1,0:T(8,128)(2,1)} %param.18), kind=kOutput, calls=%fused_computation.27 | convolution fusion | flops 537526272 | bytes 3407872 | tf_op jit(solution)/shard_map/dot_general | solution.py:304
  46.1 0.8 reshape.100
  46.9 1.2 fusion.28
  48.1 1.2 broadcast_in_dim.44
  49.4 7.3 %all-to-all-start.1 = ((bf16[8,1,2,2,128,128]{5,4,3,2,1,0:T(8,128)(2,1)}), bf16[8,1,2,2,128,128]{5,4,3,2,1,0:T(8,128)(2,1)}, u32[]{:S(2)}, u32[]{:S(2)}) async-start(bf16[8,1,2,2,128,128]{5,4,3,2,1,0:T(8,128)(2,1)} %broadcast_in_dim.44), calls=%async_computation.1 | async-start | bytes 2097152 | tf_op jit(solution)/shard_map/all_to_all | solution.py:23
  56.7 3.3 %multiply_convert_fusion.2 = bf16[512,256]{1,0:T(8,128)(2,1)} fusion(bf16[512,2048]{1,0:T(8,128)(2,1)} %copy-done.5, bf16[2048,256]{1,0:T(8,128)(2,1)} %param.16), kind=kOutput, calls=%fused_computation.26 | convolution fusion | flops 537526272 | bytes 3407872 | tf_op jit(solution)/shard_map/dot_general | solution.py:304
  60.0 1.7 reshape.101
  61.7 10.2 %all-to-all-done.1 = bf16[8,1,2,2,128,128]{5,4,3,2,1,0:T(8,128)(2,1)} async-done(((bf16[8,1,2,2,128,128]{5,4,3,2,1,0:T(8,128)(2,1)}), bf16[8,1,2,2,128,128]{5,4,3,2,1,0:T(8,128)(2,1)}, u32[]{:S(2)}, u32[]{:S(2)}) %all-to-all-start.1) | async-done | bytes 1048608 | tf_op jit(solution)/shard_map/all_to_all | solution.py:23
  71.9 1.5 fusion
  73.4 2.0 %fusion.22 = f32[2,2,128,256]{3,2,1,0:T(8,128)} fusion(bf16[2,256,2,128]{3,2,1,0:T(2,128)(2,1)} %reshape.101, f32[2,2,128,128]{3,2,1,0:T(8,128)S(1)} %fusion, f32[2,2,128,128]{3,2,1,0:T(8,128)S(1)} %get-tuple-element.6), kind=kOutput, calls=%fused_computation.38 | convolution fusion | flops 33751040 | bytes 1310720 | tf_op jit(solution)/shard_map/snihd,snhde->snihe/dot_general | solution.py:330
  75.4 0.0 copy-start.8
  75.4 2.6 %multiply_reduce_fusion.1 = (f32[2,256,2]{1,2,0:T(2,128)S(1)}, f32[2,1,256,2,128]{2,4,3,0,1:T(8,128)}) fusion(f32[2,2,128,256]{3,2,1,0:T(8,128)} %fusion.22, bf16[2,256,2,128]{1,3,2,0:T(8,128)(2,1)} %copy.34, pred[256,256]{1,0:T(8,128)(4,1)S(1)} %iota_compare_fusion, bf16[2,256,2,128]{3,2,1,0:T(2,128)(2,1)} %reshape.101, bf16[2,256,2,128]{3,2,1,0:T(2,128)(2,1)} %reshape.100), kind=kOutput, calls=%fused_computation.23 | convolution fusion | flops 135134208 | bytes 1904640 | tf_op jit(solution)/shard_map/snhij,snjhd->snihd/dot_general | solution.py:316
  78.0 0.1 copy.39
  78.1 2.1 %copy.38 = f32[2,1,256,2,128]{4,3,2,0,1:T(2,128)} copy(f32[2,1,256,2,128]{2,4,3,0,1:T(8,128)} %get-tuple-element.8) | data formatting | bytes 1048576 | tf_op jit(solution)/shard_map/add | solution.py:333
  80.2 1.4 mul.70
  81.6 0.0 copy-done
  81.6 0.0 copy-done.8
  81.6 5.8 %convolution_convert_fusion = bf16[512,2048]{1,0:T(8,128)(2,1)} fusion(bf16[256,2048]{1,0:T(8,128)(2,1)S(1)} %copy-done, bf16[512,2048]{1,0:T(8,128)(2,1)} %copy-done.5, bf16[2048,256]{1,0:T(8,128)(2,1)} %param.19, f32[64,8,2,128]{3,2,1,0:T(2,128)} %bitcast.66, f32[64,8,2,128]{3,2,1,0:T(2,128)} %bitcast.67, f32[256]{0:T(256)S(1)} %copy-done.8), kind=kOutput, calls=%fused_computation.3 | convolution fusion | flops 1075707904 | bytes 7341056 | tf_op jit(solution)/shard_map/dot_general | solution.py:340
  87.4 0.0 copy-start.1
  87.4 4.7 %all-to-all-start.2 = ((bf16[16,32,2048]{2,1,0:T(8,128)(2,1)}), bf16[16,32,2048]{2,1,0:T(8,128)(2,1)}, u32[]{:S(2)}, u32[]{:S(2)}) async-start(bf16[16,32,2048]{2,1,0:T(8,128)(2,1)} %bitcast.65), calls=%async_computation.2 | async-start | bytes 4194304 | tf_op jit(solution)/shard_map/all_to_all | solution.py:37
  92.1 0.0 copy-done.1
  92.2 0.1 copy.40.picks_ref
  92.2 1.9 copy.72
  94.1 0.0 copy-start.3
  94.1 0.0 copy-start.4
  94.1 28.9 %all-to-all-done.2 = bf16[16,32,2048]{2,1,0:T(8,128)(2,1)} async-done(((bf16[16,32,2048]{2,1,0:T(8,128)(2,1)}), bf16[16,32,2048]{2,1,0:T(8,128)(2,1)}, u32[]{:S(2)}, u32[]{:S(2)}) %all-to-all-start.2) | async-done | bytes 2097184 | tf_op jit(solution)/shard_map/all_to_all | solution.py:37
  123.0 2.0 %convert_reduce_fusion = f32[32,2048]{1,0:T(8,128)S(1)} fusion(bf16[16,32,2048]{2,1,0:T(8,128)(2,1)} %all-to-all-done.2), kind=kLoop, calls=%fused_computation | loop fusion | flops 2031616 | bytes 2359296 | tf_op jit(solution)/shard_map/reduce_sum | solution.py:38
  125.0 0.9 convert_add_fusion.residual_ref
  126.0 0.0 copy-done.3
  126.0 0.0 copy-done.4
  126.0 0.0 copy-start.2
  126.0 1.9 %copy-done.2 = bf16[1,2048,768]{2,1,0:T(8,128)(2,1)S(1)} copy-done((bf16[1,2048,768]{2,1,0:T(8,128)(2,1)S(1)}, bf16[1,2048,768]{2,1,0:T(8,128)(2,1)}, u32[]{:S(2)}) %copy-start.2) | copy-done | bytes 3145752
  127.9 57.4 %shard_map.136 = f32[32,2048]{1,0:T(8,128)S(1)} custom-call(f32[32,2048]{1,0:T(8,128)S(1)} %convert_add_fusion.residual_ref, f32[1,2048]{1,0:T(1,128)S(1)} %bitcast.60, bf16[2048,128]{1,0:T(8,128)(2,1)S(1)} %copy-done.3, s32[32,8]{1,0:T(8,128)S(1)} %copy.40.picks_ref, s32[8,32]{1,0:T(8,128)S(1)} %bitcast.58, bf16[2048,768]{1,0:T(8,128)(2,1)S(1)} %bitcast.59, ...), custom_call_target="tpu_custom_call" | custom-call | flops 3623878656 | bytes 10485760 | tf_op jit(solution)/shard_map/pallas_call | solution.py:249
  185.2 0.7 add_bitcast_fusion
  (5 shorter events, 0.1 us)
Async XLA Ops:
  0.0 81.6 %copy-start = (bf16[256,2048]{1,0:T(8,128)(2,1)S(1)}, bf16[256,2048]{1,0:T(8,128)(2,1)}, u32[]{:S(2)}) copy-start(bf16[256,2048]{1,0:T(8,128)(2,1)} %param.21) | copy-start | bytes 3145732
  37.6 0.7 copy-start.6
  38.3 2.0 %copy-start.7 = (bf16[2048,256]{1,0:T(8,128)(2,1)S(1)}, bf16[2048,256]{1,0:T(8,128)(2,1)}, u32[]{:S(2)}) copy-start(bf16[2048,256]{1,0:T(8,128)(2,1)} %param.17) | copy-start | bytes 3145732
  38.9 1.3 copy-start.5
  49.4 22.5 %all-to-all-start.1 = ((bf16[8,1,2,2,128,128]{5,4,3,2,1,0:T(8,128)(2,1)}), bf16[8,1,2,2,128,128]{5,4,3,2,1,0:T(8,128)(2,1)}, u32[]{:S(2)}, u32[]{:S(2)}) async-start(bf16[8,1,2,2,128,128]{5,4,3,2,1,0:T(8,128)(2,1)} %broadcast_in_dim.44), calls=%async_computation.1 | async-start | bytes 2097152 | tf_op jit(solution)/shard_map/all_to_all | solution.py:23
  75.4 6.2 %copy-start.8 = (f32[256]{0:T(256)S(1)}, f32[256]{0:T(256)}, u32[]{:S(2)}) copy-start(f32[256]{0:T(256)} %param.20) | copy-start | bytes 3076
  87.4 4.8 %copy-start.1 = (s32[1,32,8]{1,2,0:T(8,128)S(1)}, s32[1,32,8]{1,2,0:T(8,128)}, u32[]{:S(2)}) copy-start(s32[1,32,8]{1,2,0:T(8,128)} %param.24) | copy-start | bytes 3076
  87.4 35.6 %all-to-all-start.2 = ((bf16[16,32,2048]{2,1,0:T(8,128)(2,1)}), bf16[16,32,2048]{2,1,0:T(8,128)(2,1)}, u32[]{:S(2)}, u32[]{:S(2)}) async-start(bf16[16,32,2048]{2,1,0:T(8,128)(2,1)} %bitcast.65), calls=%async_computation.2 | async-start | bytes 4194304 | tf_op jit(solution)/shard_map/all_to_all | solution.py:37
  94.1 31.9 %copy-start.3 = (bf16[2048,128]{1,0:T(8,128)(2,1)S(1)}, bf16[2048,128]{1,0:T(8,128)(2,1)}, u32[]{:S(2)}) copy-start(bf16[2048,128]{1,0:T(8,128)(2,1)} %router_ref.1) | copy-start | bytes 1572868
  94.1 31.9 %copy-start.4 = (f32[2048]{0:T(1024)S(1)}, f32[2048]{0:T(1024)}, u32[]{:S(2)}) copy-start(f32[2048]{0:T(1024)} %param.22) | copy-start | bytes 24580
  126.0 1.9 %copy-start.2 = (bf16[1,2048,768]{2,1,0:T(8,128)(2,1)S(1)}, bf16[1,2048,768]{2,1,0:T(8,128)(2,1)}, u32[]{:S(2)}) copy-start(bf16[1,2048,768]{2,1,0:T(8,128)(2,1)} %param.25) | copy-start | bytes 9437188

commit v2 on v1

v2 whole, which is shorter than its diff:
```python
import jax
import jax.numpy as jnp
from jax import lax
from jax.experimental import pallas as pl
from jax.experimental.pallas import tpu as pltpu
from jax.sharding import PartitionSpec as P

MESH = pl.DeviceIdType.MESH
SEQ = 8
HEAD = 16
DEVS = SEQ * HEAD
DH = 128
BLOCK = 256
ROWS = 32
TOP = 8
SLOTS = 3
WIDTH = 2048
HIDDEN = 768
TILES = WIDTH // 128
CHUNK = SLOTS * TILES
HALF = DEVS // 2
HERE = 256
WIDE = WIDTH // 2
PIECE = WIDE // 2
FAR_FIRST = (2, 3, 1, 0)

epsilon = 1e-06


def rms_scale(values, gain_vec):
    mean_sq = jnp.mean(values * values, axis=-1, keepdims=True)
    return values * lax.rsqrt(mean_sq + epsilon) * gain_vec


def dot(a, b):
    return jnp.dot(a, b, preferred_element_type=jnp.float32)


def arrived_in(ref, sem):
    pltpu.make_async_copy(ref, ref, sem).wait()


def layer_kernel(
    tokens_hbm,
    attn_gain_hbm,
    query_hbm,
    key_hbm,
    value_hbm,
    gate_hbm,
    head_gain_hbm,
    out_hbm,
    moe_gain_hbm,
    router_hbm,
    picks_hbm,
    exp_gate_hbm,
    exp_up_hbm,
    exp_down_hbm,
    layer_out,
    attn_gain,
    w_query,
    w_key,
    w_value,
    w_gate,
    head_gain,
    w_out,
    moe_gain,
    w_router,
    picks_ref,
    gate_w,
    up_w,
    down_w,
    gathered,
    squares,
    acc,
    keys,
    values,
    states,
    pair_out,
    pair_in,
    total_out,
    total_in,
    prefix_out,
    prefix_in,
    mixed,
    gated,
    partial,
    near_sum,
    s1,
    r1,
    s2,
    r2,
    s3,
    r3,
    s4,
    r4,
    select,
    match_ref,
    before_ref,
    residual_ref,
    spread,
    outgoing,
    arrived,
    result,
    returned,
    rows,
    load_sem,
    own_sem,
    gather_out,
    first_in,
    second_in,
    state_out,
    state_in,
    sum_out,
    sum1_in,
    sum2_in,
    sum3_in,
    sum4_in,
    out_sem,
    in_sem,
    back_out_sem,
    back_in_sem,
):
    my_seq = lax.axis_index("seq")
    my_head = lax.axis_index("head")
    me = my_seq * HEAD + my_head
    my_x = lax.rem(my_head, 4)
    my_y = my_head // 4
    my_z = my_seq // 2
    my_core = lax.rem(my_seq, 2)
    other_core = my_seq + 1 - 2 * my_core

    def head_at(t, first, second):
        dx, dy = (first, second) if t == 0 else (second, first)
        return lax.rem(my_y + dy, 4) * 4 + lax.rem(my_x + dx, 4)

    barrier = pltpu.get_barrier_semaphore()
    partners = [(my_seq, head_at(0, 1, 0)), (my_seq, head_at(0, 3, 0))]
    partners += [(my_seq, head_at(0, 0, 1)), (my_seq, head_at(0, 0, 3))]
    partners += [(other_core, my_head)]
    partners += [(lax.rem(my_z + dz, 4) * 2 + my_core, my_head) for dz in (1, 2, 3)]
    for partner in partners:
        pl.semaphore_signal(barrier, inc=1, device_id=partner, device_id_type=MESH)
    own = pltpu.make_async_copy(tokens_hbm, gathered.at[my_head], own_sem)
    own.start()
    loads = [
        pltpu.make_async_copy(hbm, vmem, load_sem.at[i])
        for i, (hbm, vmem) in enumerate(
            (
                (attn_gain_hbm, attn_gain),
                (query_hbm, w_query),
                (key_hbm, w_key),
                (value_hbm, w_value),
                (gate_hbm, w_gate),
                (picks_hbm, picks_ref),
                (head_gain_hbm, head_gain),
                (out_hbm, w_out),
                (moe_gain_hbm, moe_gain),
                (router_hbm, w_router),
                (exp_gate_hbm, gate_w),
                (exp_up_hbm, up_w),
                (exp_down_hbm, down_w),
            )
        )
    ]
    for load in loads:
        load.start()
    pl.semaphore_wait(barrier, len(partners))

    def push(source, target, t, first, second, send_sem, recv_sem):
        pltpu.make_async_remote_copy(
            src_ref=source,
            dst_ref=target,
            send_sem=send_sem,
            recv_sem=recv_sem,
            device_id=(my_seq, head_at(t, first, second)),
            device_id_type=MESH,
        ).start()

    def block(t, first, second):
        return gathered.at[head_at(t, first, second), t]

    def part(ref, i):
        return ref.at[pl.ds(i * BLOCK // 2, BLOCK // 2)]

    def pass_on(t, first, source):
        here = block(t, first, 0)
        push(source, here, t, 0, 1, gather_out, second_in.at[t, first, 0])
        push(source, here, t, 0, 3, gather_out, second_in.at[t, first, 1])

    for t in range(2):
        mine = block(t, 0, 0)
        push(tokens_hbm.at[t], mine, t, 1, 0, gather_out, first_in.at[t, 0])
        push(tokens_hbm.at[t], mine, t, 3, 0, gather_out, first_in.at[t, 1])
        pass_on(t, 0, tokens_hbm.at[t])

    loads[5].wait()
    picks = picks_ref[0]
    lane = lax.broadcasted_iota(jnp.int32, (ROWS, DEVS), 1)
    match = jnp.zeros((ROWS, DEVS), jnp.float32)
    for k in range(TOP):
        match = match + jnp.where(picks[:, k : k + 1] == lane, 1.0, 0.0)
    row_i = lax.broadcasted_iota(jnp.int32, (ROWS, ROWS), 0)
    col_i = lax.broadcasted_iota(jnp.int32, (ROWS, ROWS), 1)
    earlier = jnp.where(col_i < row_i, 1.0, 0.0).astype(jnp.bfloat16)
    before = dot(earlier, match.astype(jnp.bfloat16))
    match_ref[...] = match
    before_ref[...] = before
    for c in range(SLOTS):
        select[c * DEVS : (c + 1) * DEVS, :] = jnp.transpose(
            jnp.where(before == float(c), match, 0.0)
        ).astype(jnp.bfloat16)

    for t in range(2):
        arrived_in(block(t, 3, 0), first_in.at[t, 0])
        push(part(block(t, 3, 0), 0), part(block(t, 3, 0), 0), t, 1, 0, gather_out, first_in.at[t, 2])
        pass_on(t, 3, block(t, 3, 0))
        arrived_in(block(t, 1, 0), first_in.at[t, 1])
        push(part(block(t, 1, 0), 1), part(block(t, 1, 0), 1), t, 3, 0, gather_out, first_in.at[t, 3])
        pass_on(t, 1, block(t, 1, 0))
    for t in range(2):
        arrived_in(part(block(t, 2, 0), 0), first_in.at[t, 2])
        arrived_in(part(block(t, 2, 0), 1), first_in.at[t, 3])
        pass_on(t, 2, block(t, 2, 0))

    own.wait()
    for i in range(5):
        loads[i].wait()
    weights_in = (w_query, w_key, w_value, w_gate)

    def project_line(t, second):
        heads = [head_at(t, first, second) for first in range(4)]
        total = None
        pieces = []
        for h in heads:
            piece = gathered[h, t].astype(jnp.float32)
            square = piece * piece
            total = square if total is None else total + square
            pieces.append((piece * attn_gain[pl.ds(h, 1), :]).astype(jnp.bfloat16))
        if second == 0:
            squares[t] = total
        else:
            squares[t] += total
        line = jnp.concatenate(pieces, axis=1)
        for i, weight in enumerate(weights_in):
            deep = jnp.concatenate(
                [weight[pl.ds(pl.multiple_of(h * 128, 128), 128), :] for h in heads], axis=0
            )
            product = dot(line, deep)
            if second == 0:
                acc[t, :, i * HERE : (i + 1) * HERE] = product
            else:
                acc[t, :, i * HERE : (i + 1) * HERE] += product

    def forward_line(t):
        for first in (0, 3, 1, 2):
            lower = block(t, first, 3)
            arrived_in(lower, second_in.at[t, first, 0])
            push(part(lower, 0), part(lower, 0), t, 0, 1, gather_out, second_in.at[t, first, 2])
            upper = block(t, first, 1)
            arrived_in(upper, second_in.at[t, first, 1])
            push(part(upper, 1), part(upper, 1), t, 0, 3, gather_out, second_in.at[t, first, 3])

    project_line(0, 0)
    project_line(1, 0)
    forward_line(0)
    forward_line(1)
    for t in range(2):
        project_line(t, 3)
        project_line(t, 1)
    for t in range(2):
        for first in (0, 3, 1, 2):
            arrived_in(part(block(t, first, 2), 0), second_in.at[t, first, 2])
            arrived_in(part(block(t, first, 2), 1), second_in.at[t, first, 3])
        project_line(t, 2)

    def scale_of(t):
        mean_sq = jnp.sum(squares[t], axis=-1, keepdims=True) * (1.0 / WIDTH)
        return lax.rsqrt(mean_sq + epsilon)

    for t in range(2):
        scale = scale_of(t)
        keys[t] = jax.nn.silu(acc[t, :, HERE : 2 * HERE] * scale).astype(jnp.bfloat16)
        values[t] = jax.nn.silu(acc[t, :, 2 * HERE : 3 * HERE] * scale).astype(jnp.bfloat16)
        for h in range(2):
            states[t, h] = lax.dot_general(
                keys[t, :, h * DH : (h + 1) * DH],
                values[t, :, h * DH : (h + 1) * DH],
                (((0,), (0,)), ((), ())),
                preferred_element_type=jnp.float32,
            )
    pair_out[...] = states[1 - my_core].astype(jnp.bfloat16)
    pair = pltpu.make_async_remote_copy(
        src_ref=pair_out,
        dst_ref=pair_in,
        send_sem=state_out.at[0],
        recv_sem=state_in.at[0],
        device_id=(other_core, my_head),
        device_id_type=MESH,
    )
    pair.start()

    causal = lax.broadcasted_iota(jnp.int32, (BLOCK, BLOCK), 0) >= lax.broadcasted_iota(
        jnp.int32, (BLOCK, BLOCK), 1
    )

    def inner(t):
        queries = jax.nn.silu(acc[t, :, 0:HERE] * scale_of(t)).astype(jnp.bfloat16)
        gated[t] = queries
        for h in range(2):
            cols = slice(h * DH, (h + 1) * DH)
            scores = lax.dot_general(
                queries[:, cols],
                keys[t, :, cols],
                (((1,), (1,)), ((), ())),
                preferred_element_type=jnp.float32,
            )
            scores = jnp.where(causal, scores, 0.0).astype(jnp.bfloat16)
            mixed[t, :, cols] = dot(scores, values[t, :, cols])

    pair.wait_recv()
    total_out[...] = (states[my_core] + pair_in[...].astype(jnp.float32)).astype(jnp.bfloat16)
    totals = [
        pltpu.make_async_remote_copy(
            src_ref=total_out,
            dst_ref=total_in.at[dz - 1],
            send_sem=state_out.at[dz],
            recv_sem=state_in.at[dz],
            device_id=(lax.rem(my_z + dz, 4) * 2 + my_core, my_head),
            device_id_type=MESH,
        )
        for dz in (1, 2, 3)
    ]
    for total in totals:
        total.start()
    inner(0)
    inner(1)
    base = jnp.zeros((2, DH, DH), jnp.float32)
    for dz in (1, 2, 3):
        totals[dz - 1].wait_recv()
        earlier_chip = jnp.where(my_z >= dz, 1.0, 0.0)
        base = base + earlier_chip * total_in[dz - 1].astype(jnp.float32)
    second_core = my_core.astype(jnp.float32)
    prefix_out[1] = (base + second_core * pair_in[...].astype(jnp.float32)).astype(jnp.bfloat16)
    prefix_out[0] = (base + (1.0 - second_core) * states[my_core]).astype(jnp.bfloat16)
    hand_over = pltpu.make_async_remote_copy(
        src_ref=prefix_out.at[0],
        dst_ref=prefix_in,
        send_sem=state_out.at[4],
        recv_sem=state_in.at[4],
        device_id=(other_core, my_head),
        device_id_type=MESH,
    )
    hand_over.start()
    for i in (6, 7):
        loads[i].wait()
    hand_over.wait_recv()

    for t in range(2):
        gate = jax.nn.sigmoid(acc[t, :, 3 * HERE : 4 * HERE] * scale_of(t))
        for h in range(2):
            cols = slice(h * DH, (h + 1) * DH)
            prefix = jnp.where(my_core == t, prefix_out[1, h], prefix_in[h])
            whole = mixed[t, :, cols] + dot(gated[t, :, cols], prefix)
            normed = rms_scale(whole, head_gain[h : h + 1, :])
            gated[t, :, cols] = (normed * gate[:, cols]).astype(jnp.bfloat16)
    for t in range(2):
        for j in range(4):
            cols = slice(j * 512, (j + 1) * 512)
            partial[t * BLOCK : (t + 1) * BLOCK, cols] = dot(gated[t], w_out[:, cols])

    def own_part(t, first, second, low, high):
        start = pl.multiple_of(head_at(t, first, second) * ROWS, ROWS)
        return partial[pl.ds(start, ROWS), t * WIDE + low : t * WIDE + high]

    for k in FAR_FIRST:
        for t in range(2):
            s1[t, k, 0] = own_part(t, k, 2, 0, PIECE).astype(jnp.bfloat16)
            push(s1.at[t, k, 0], r1.at[t, k, 0], t, 0, 1, sum_out.at[0], sum1_in.at[t, k, 0])
            s1[t, k, 1] = own_part(t, k, 2, PIECE, WIDE).astype(jnp.bfloat16)
            push(s1.at[t, k, 1], r1.at[t, k, 1], t, 0, 3, sum_out.at[0], sum1_in.at[t, k, 1])
    for k in FAR_FIRST:
        for t in range(2):
            arrived_in(r1.at[t, k, 0], sum1_in.at[t, k, 0])
            s2[t, k, 0, :, 0:PIECE] = (
                own_part(t, k, 1, 0, PIECE) + r1[t, k, 0].astype(jnp.float32)
            ).astype(jnp.bfloat16)
            s2[t, k, 0, :, PIECE:WIDE] = own_part(t, k, 1, PIECE, WIDE).astype(jnp.bfloat16)
            push(s2.at[t, k, 0], r2.at[t, k, 0], t, 0, 1, sum_out.at[1], sum2_in.at[t, k, 0])
            arrived_in(r1.at[t, k, 1], sum1_in.at[t, k, 1])
            s2[t, k, 1, :, 0:PIECE] = own_part(t, k, 3, 0, PIECE).astype(jnp.bfloat16)
            s2[t, k, 1, :, PIECE:WIDE] = (
                own_part(t, k, 3, PIECE, WIDE) + r1[t, k, 1].astype(jnp.float32)
            ).astype(jnp.bfloat16)
            push(s2.at[t, k, 1], r2.at[t, k, 1], t, 0, 3, sum_out.at[1], sum2_in.at[t, k, 1])
    for k in FAR_FIRST:
        for t in range(2):
            arrived_in(r2.at[t, k, 0], sum2_in.at[t, k, 0])
            arrived_in(r2.at[t, k, 1], sum2_in.at[t, k, 1])
            line_sum = (
                own_part(t, k, 0, 0, WIDE)
                + r2[t, k, 0].astype(jnp.float32)
                + r2[t, k, 1].astype(jnp.float32)
            )
            if k == 2:
                s3[t, 0] = line_sum[:, :PIECE].astype(jnp.bfloat16)
                push(s3.at[t, 0], r3.at[t, 0], t, 1, 0, sum_out.at[2], sum3_in.at[t, 0])
                s3[t, 1] = line_sum[:, PIECE:].astype(jnp.bfloat16)
                push(s3.at[t, 1], r3.at[t, 1], t, 3, 0, sum_out.at[2], sum3_in.at[t, 1])
            else:
                near_sum[t, k] = line_sum
    for t in range(2):
        arrived_in(r3.at[t, 0], sum3_in.at[t, 0])
        s4[t, 0, :, 0:PIECE] = (
            near_sum[t, 1, :, 0:PIECE] + r3[t, 0].astype(jnp.float32)
        ).astype(jnp.bfloat16)
        s4[t, 0, :, PIECE:WIDE] = near_sum[t, 1, :, PIECE:WIDE].astype(jnp.bfloat16)
        push(s4.at[t, 0], r4.at[t, 0], t, 1, 0, sum_out.at[3], sum4_in.at[t, 0])
        arrived_in(r3.at[t, 1], sum3_in.at[t, 1])
        s4[t, 1, :, 0:PIECE] = near_sum[t, 3, :, 0:PIECE].astype(jnp.bfloat16)
        s4[t, 1, :, PIECE:WIDE] = (
            near_sum[t, 3, :, PIECE:WIDE] + r3[t, 1].astype(jnp.float32)
        ).astype(jnp.bfloat16)
        push(s4.at[t, 1], r4.at[t, 1], t, 3, 0, sum_out.at[3], sum4_in.at[t, 1])
    own_start = pl.multiple_of(lax.rem(my_head, 8) * ROWS, ROWS)
    for j in range(TILES):
        residual_ref[:, j * 128 : (j + 1) * 128] = gathered[
            j, my_head // 8, pl.ds(own_start, ROWS), :
        ].astype(jnp.float32)
    for t in range(2):
        arrived_in(r4.at[t, 0], sum4_in.at[t, 0])
        arrived_in(r4.at[t, 1], sum4_in.at[t, 1])
        residual_ref[:, t * WIDE : (t + 1) * WIDE] += (
            near_sum[t, 0] + r4[t, 0].astype(jnp.float32) + r4[t, 1].astype(jnp.float32)
        )

    for i in (8, 9):
        loads[i].wait()
    moe_in = rms_scale(residual_ref[...], moe_gain[...]).astype(jnp.bfloat16)
    for j in range(0, TILES, 2):
        picked = dot(select[...], moe_in[:, j * 128 : (j + 2) * 128])
        for c in range(SLOTS):
            for half in range(2):
                spread[pl.ds(c * TILES + j + half, DEVS, CHUNK), :] = picked[
                    c * DEVS : (c + 1) * DEVS, half * 128 : (half + 1) * 128
                ]
    for o in range(SEQ):
        to_seq = lax.rem(my_seq + o, SEQ)
        start = pl.multiple_of(to_seq * (HEAD * CHUNK), HEAD * CHUNK)
        outgoing[pl.ds(to_seq * HEAD, HEAD)] = (
            spread[pl.ds(start, HEAD * CHUNK), :].astype(jnp.bfloat16).reshape(HEAD, CHUNK, 128)
        )

        def send(i, carry):
            to_head = lax.rem(my_head + i, HEAD)
            pltpu.make_async_remote_copy(
                src_ref=outgoing.at[to_seq * HEAD + to_head],
                dst_ref=arrived.at[o * HEAD + my_head],
                send_sem=out_sem,
                recv_sem=in_sem.at[o],
                device_id=(to_seq, to_head),
                device_id_type=MESH,
            ).start()
            return carry

        if o == 0:
            pltpu.make_async_copy(outgoing.at[me], arrived.at[my_head], in_sem.at[0]).start()
        lax.fori_loop(1 if o == 0 else 0, HEAD, send, 0)

    logits = dot(moe_in, w_router[...])
    scores = match_ref[...] * jax.nn.sigmoid(logits)
    weights = scores / jnp.sum(scores, axis=1, keepdims=True)
    before = before_ref[...]
    spread_weights = jnp.concatenate(
        [jnp.where(before == float(c), weights, 0.0) for c in range(SLOTS)], axis=1
    )
    high = spread_weights.astype(jnp.bfloat16)
    low = (spread_weights - high.astype(jnp.float32)).astype(jnp.bfloat16)
    combine = jnp.concatenate([high, low], axis=0)

    for i in (10, 11, 12):
        loads[i].wait()
    part_rows = HALF * SLOTS
    for p in range(2):
        for o in range(p * SEQ // 2, (p + 1) * SEQ // 2):
            group = arrived.at[pl.ds(o * HEAD, HEAD)]
            arrived_in(group, in_sem.at[o])
        for q in range(4):
            chunk = arrived[pl.ds(p * HALF + q * HEAD, HEAD)]
            spread[pl.ds(q * HEAD * CHUNK, HEAD * CHUNK), :] = chunk.astype(jnp.float32).reshape(
                HEAD * CHUNK, 128
            )
        for j in range(TILES):
            rows[0:part_rows, j * 128 : (j + 1) * 128] = spread[
                pl.ds(j, part_rows, TILES), :
            ].astype(jnp.bfloat16)
        inputs = rows[0:part_rows, :]
        hidden = (jax.nn.silu(dot(inputs, gate_w[...])) * dot(inputs, up_w[...])).astype(
            jnp.bfloat16
        )
        for j in range(0, TILES, 2):
            produced = dot(hidden, down_w[:, j * 128 : (j + 2) * 128])
            for half in range(2):
                spread[pl.ds(j + half, part_rows, TILES), :] = produced[
                    :, half * 128 : (half + 1) * 128
                ]
        for o in range(p * SEQ // 2, (p + 1) * SEQ // 2):
            q = o - p * SEQ // 2
            result[pl.ds(o * HEAD, HEAD)] = (
                spread[pl.ds(q * HEAD * CHUNK, HEAD * CHUNK), :]
                .astype(jnp.bfloat16)
                .reshape(HEAD, CHUNK, 128)
            )
            to_seq = lax.rem(my_seq + SEQ - o, SEQ)

            def send_back(i, carry):
                to_head = lax.rem(my_head + i, HEAD)
                pltpu.make_async_remote_copy(
                    src_ref=result.at[o * HEAD + to_head],
                    dst_ref=returned.at[me],
                    send_sem=back_out_sem,
                    recv_sem=back_in_sem,
                    device_id=(to_seq, to_head),
                    device_id_type=MESH,
                ).start()
                return carry

            if o == 0:
                pltpu.make_async_copy(result.at[my_head], returned.at[me], back_in_sem).start()
            lax.fori_loop(1 if o == 0 else 0, HEAD, send_back, 0)

    arrived_in(returned, back_in_sem)
    for q in range(SEQ):
        spread[pl.ds(q * HEAD * CHUNK, HEAD * CHUNK), :] = (
            returned[pl.ds(q * HEAD, HEAD)].astype(jnp.float32).reshape(HEAD * CHUNK, 128)
        )
    for c in range(SLOTS):
        for j in range(TILES):
            rows[c * DEVS : (c + 1) * DEVS, j * 128 : (j + 1) * 128] = spread[
                pl.ds(c * TILES + j, DEVS, CHUNK), :
            ].astype(jnp.bfloat16)
    both = dot(combine, rows[...])
    layer_out[0] = residual_ref[...] + both[:ROWS] + both[ROWS:]

    sent = gathered.at[pl.ds(0, HEAD - 1)]
    pltpu.make_async_copy(sent, sent, gather_out).wait()
    pair.wait_send()
    for total in totals:
        total.wait_send()
    hand_over.wait_send()
    for i, ref in enumerate((s1, s2, s3, s4)):
        pltpu.make_async_copy(ref, ref, sum_out.at[i]).wait()
    sent = outgoing.at[pl.ds(0, DEVS - 1)]
    pltpu.make_async_copy(sent, sent, out_sem).wait()
    sent = result.at[pl.ds(0, DEVS - 1)]
    pltpu.make_async_copy(sent, sent, back_out_sem).wait()


def local(
    tokens,
    attn_gain,
    w_query,
    w_key,
    w_value,
    w_gate,
    head_gain,
    w_out,
    moe_gain,
    w_router,
    expert_picks,
    exp_gate,
    exp_up,
    exp_down,
):
    args = (
        tokens,
        attn_gain.reshape(TILES, 128),
        w_query,
        w_key,
        w_value,
        w_gate,
        head_gain.reshape(2, DH),
        w_out,
        moe_gain.reshape(1, WIDTH),
        w_router,
        expert_picks,
        exp_gate[0],
        exp_up[0],
        exp_down[0],
    )

    def half(*shape):
        return pltpu.VMEM(shape, jnp.bfloat16)

    def full(*shape):
        return pltpu.VMEM(shape, jnp.float32)

    def sems(*shape):
        return pltpu.SemaphoreType.DMA(shape)

    return pl.pallas_call(
        layer_kernel,
        out_shape=jax.ShapeDtypeStruct((1, ROWS, WIDTH), jnp.float32),
        in_specs=[pl.BlockSpec(memory_space=pl.ANY)] * len(args),
        out_specs=pl.BlockSpec(memory_space=pltpu.VMEM),
        scratch_shapes=[pltpu.VMEM(a.shape, a.dtype) for a in args[1:]]
        + [
            half(HEAD, 2, BLOCK, 128),
            full(2, BLOCK, 128),
            full(2, BLOCK, 4 * HERE),
            half(2, BLOCK, HERE),
            half(2, BLOCK, HERE),
            full(2, 2, DH, DH),
            half(2, DH, DH),
            half(2, DH, DH),
            half(2, DH, DH),
            half(3, 2, DH, DH),
            half(2, 2, DH, DH),
            half(2, DH, DH),
            full(2, BLOCK, HERE),
            half(2, BLOCK, HERE),
            full(2 * BLOCK, WIDTH),
            full(2, 4, ROWS, WIDE),
            half(2, 4, 2, ROWS, PIECE),
            half(2, 4, 2, ROWS, PIECE),
            half(2, 4, 2, ROWS, WIDE),
            half(2, 4, 2, ROWS, WIDE),
            half(2, 2, ROWS, PIECE),
            half(2, 2, ROWS, PIECE),
            half(2, 2, ROWS, WIDE),
            half(2, 2, ROWS, WIDE),
            half(DEVS * SLOTS, ROWS),
            full(ROWS, DEVS),
            full(ROWS, DEVS),
            full(ROWS, WIDTH),
            full(DEVS * CHUNK, 128),
            half(DEVS, CHUNK, 128),
            half(DEVS, CHUNK, 128),
            half(DEVS, CHUNK, 128),
            half(DEVS, CHUNK, 128),
            half(DEVS * SLOTS, WIDTH),
            sems(13),
            sems(),
            sems(),
            sems(2, 4),
            sems(2, 4, 4),
            sems(5),
            sems(5),
            sems(4),
            sems(2, 4, 2),
            sems(2, 4, 2),
            sems(2, 2),
            sems(2, 2),
            sems(),
            sems(SEQ),
            sems(),
            sems(),
        ],
        compiler_params=pltpu.CompilerParams(
            collective_id=1, has_side_effects=True, vmem_limit_bytes=56 * 1024 * 1024
        ),
        cost_estimate=pl.CostEstimate(
            flops=7 << 30, bytes_accessed=20 << 20, transcendentals=0
        ),
    )(*args)


def solution(mesh):
    placed = (
        P(None, "seq", "head"),
        P(),
        P(None, "head"),
        P(None, "head"),
        P(None, "head"),
        P(None, "head"),
        P("head"),
        P("head", None),
        P(),
        P(),
        P("seq", "head", None),
        P(("seq", "head"), None, None),
        P(("seq", "head"), None, None),
        P(("seq", "head"), None, None),
    )
    return jax.shard_map(
        local, mesh=mesh, in_specs=placed, out_specs=P("seq", "head", None), check_vma=False
    )
```

time: 189 us -> 99.5 us (0.53); the launches traced: 186 us -> 99.2 us
  waiting for transfers between devices: 39.1 us -> 0 us
  Pallas kernels: 57.4 us -> 96.2 us
  blocking collectives: 34.7 us -> 0 us
  matrix products: 18.9 us -> 0 us
  local copies, waits for them, and re-layouts: 17.4 us -> 3.04 us
  starting transfers between devices: 12 us -> 0 us
  other arithmetic: 6.35 us -> 0 us
    all_to_all x2 -> x0, waiting for transfers between devices: 39.1 us -> none  [the longest x1 28.9 us: summed_on_arrival(): lax.all_to_all(pieces, axis, split_axis=0, concat_axis=0, tiled=True)]
    pallas_call x1, Pallas kernels: 57.4 us -> 96.2 us  [local(): pl.pallas_call(layer_kernel, out_shape=jax.ShapeDtypeStruct((1, ROWS, WID...]
    all_to_all x1 -> x0, blocking collectives: 34.7 us -> none  [from_everyone(): return lax.all_to_all(copies, axis, split_axis=0, concat_axis=0, tiled=True)]
    dot_general x7 -> x0, matrix products: 18.9 us -> none  [the longest x3 7.3 us: project(): return jnp.dot(normed, weight, preferred_element_type=jnp.float32)]
    all_to_all x2 -> x0, starting transfers between devices: 12 us -> none  [the longest x1 7.29 us: from_everyone(): return lax.all_to_all(copies, axis, split_axis=0, concat_axis=0, tiled=True)]
    reduce_sum x3 -> x0, other arithmetic: 4.01 us -> none  [the longest x1 2 us: summed_on_arrival(): return arrived.astype(jnp.float32).sum(axis=0)]
    broadcast_in_dim x2 -> x0, local copies, waits for them, and re-layouts: 2.68 us -> none  [from_everyone(): copies = jnp.broadcast_to(value, (lax.axis_size(axis), *value.shape))]
    another operation x3 -> x0, local copies, waits for them, and re-layouts: 2.64 us -> none
  transfers between devices with their start and end apart: 2 -> 0, of which waited for: 2 -> 0; matrix products, arithmetic and copies ran while one was open for 4% -> 0% of each run, Pallas kernels for 0% -> 0%
where the time goes in v2:
time: 99.5 us; the launch traced here: 99.2 us
  Pallas kernels  96.2 us (97%)
  local copies, waits for them, and re-layouts  3.04 us (3%)
    pallas_call x1, Pallas kernels, local(): pl.pallas_call(layer_kernel, out_shape=jax.ShapeDtypeStruct((1, ROWS, WID...  96.2 us
    unnamed x2, local copies, waits for them, and re-layouts  3.04 us

profile of v2, /device:TPU:1, one launch (start us, length us, event | category | flops | bytes accessed | tf_op | source)
XLA Modules:
  0.0 99.2 jit_solution(4077764897897295737)
XLA Ops:
  0.0 1.4 %copy.15.picks_hbm = s32[1,32,8]{2,1,0:T(8,128)} copy(s32[1,32,8]{1,2,0:T(8,128)} %param.24) | data formatting | bytes 2048 | tf_op args[10]
  1.4 96.2 %shard_map.136 = f32[1,32,2048]{2,1,0:T(8,128)} custom-call(bf16[2,256,128]{2,1,0:T(8,128)(2,1)} %tokens_hbm.1, f32[16,128]{1,0:T(8,128)} %bitcast.9, bf16[2048,256]{1,0:T(8,128)(2,1)} %query_hbm.1, bf16[2048,256]{1,0:T(8,128)(2,1)} %key_hbm.1, bf16[2048,256]{1,0:T(8,128)(2,1)} %value_hbm.1, bf16[2048,256]{1,0:T(8,128)(2,1)} %gate_hbm.1, f32[2,128]{1,0:T(2,128)} %bitcast.11, ...), custom_call_target="tpu_custom_call" | custom-call | flops 7516192768 | bytes 20971520 | tf_op jit(solution)/shard_map/pallas_call | solution.py:600
  97.6 1.7 %copy.17 = f32[1,32,2048]{2,1,0:T(8,128)} copy(f32[1,32,2048]{2,1,0:T(8,128)} %shard_map.136) | data formatting | bytes 524288

commit v3 on v2

--- a/solution.py
+++ b/solution.py
@@ -18,7 +18,8 @@
 HIDDEN = 768
 TILES = WIDTH // 128
 CHUNK = SLOTS * TILES
-HALF = DEVS // 2
+GROUPS = 4
+MEMBERS = DEVS // GROUPS
 HERE = 256
 WIDE = WIDTH // 2
 PIECE = WIDE // 2
@@ -55,7 +56,8 @@
     exp_gate_hbm,
     exp_up_hbm,
     exp_down_hbm,
-    layer_out,
+    residual_ref,
+    moe_ref,
     attn_gain,
     w_query,
     w_key,
@@ -91,12 +93,10 @@
     r2,
     s3,
     r3,
-    s4,
-    r4,
     select,
     match_ref,
-    before_ref,
-    residual_ref,
+    permute,
+    slot_ref,
     spread,
     outgoing,
     arrived,
@@ -114,7 +114,6 @@
     sum1_in,
     sum2_in,
     sum3_in,
-    sum4_in,
     out_sem,
     in_sem,
     back_out_sem,
@@ -136,6 +135,7 @@
     barrier = pltpu.get_barrier_semaphore()
     partners = [(my_seq, head_at(0, 1, 0)), (my_seq, head_at(0, 3, 0))]
     partners += [(my_seq, head_at(0, 0, 1)), (my_seq, head_at(0, 0, 3))]
+    partners += [(my_seq, head_at(0, 2, 0)), (my_seq, head_at(0, 0, 2))]
     partners += [(other_core, my_head)]
     partners += [(lax.rem(my_z + dz, 4) * 2 + my_core, my_head) for dz in (1, 2, 3)]
     for partner in partners:
@@ -188,71 +188,45 @@
         push(source, here, t, 0, 3, gather_out, second_in.at[t, first, 1])
 
     for t in range(2):
-        mine = block(t, 0, 0)
-        push(tokens_hbm.at[t], mine, t, 1, 0, gather_out, first_in.at[t, 0])
-        push(tokens_hbm.at[t], mine, t, 3, 0, gather_out, first_in.at[t, 1])
+        for step in (1, 3, 2):
+            push(tokens_hbm.at[t], block(t, 0, 0), t, step, 0, gather_out, first_in.at[t, 4 - step])
+    for t in range(2):
         pass_on(t, 0, tokens_hbm.at[t])
 
     loads[5].wait()
+    line = lax.broadcasted_iota(jnp.int32, (DEVS, ROWS), 0)
+    offset = line // MEMBERS
+    step_x = lax.rem(line, 4)
+    expert_x = lax.rem(my_x + step_x, 4)
+    expert_y = lax.rem(my_y + step_x + offset, 4)
+    expert_seq = lax.rem(my_seq + lax.rem(line // 4, SEQ), SEQ)
+    expert = expert_seq * HEAD + expert_y * 4 + expert_x
     picks = picks_ref[0]
-    lane = lax.broadcasted_iota(jnp.int32, (ROWS, DEVS), 1)
-    match = jnp.zeros((ROWS, DEVS), jnp.float32)
+    match_t = jnp.zeros((DEVS, ROWS), jnp.float32)
+    near_t = jnp.zeros((DEVS, ROWS), jnp.float32)
     for k in range(TOP):
-        match = match + jnp.where(picks[:, k : k + 1] == lane, 1.0, 0.0)
+        match_t = match_t + jnp.where(picks[k : k + 1, :] == line, 1.0, 0.0)
+        near_t = near_t + jnp.where(picks[k : k + 1, :] == expert, 1.0, 0.0)
     row_i = lax.broadcasted_iota(jnp.int32, (ROWS, ROWS), 0)
     col_i = lax.broadcasted_iota(jnp.int32, (ROWS, ROWS), 1)
-    earlier = jnp.where(col_i < row_i, 1.0, 0.0).astype(jnp.bfloat16)
-    before = dot(earlier, match.astype(jnp.bfloat16))
-    match_ref[...] = match
-    before_ref[...] = before
+    earlier_t = jnp.where(row_i < col_i, 1.0, 0.0).astype(jnp.bfloat16)
+    before_t = dot(near_t.astype(jnp.bfloat16), earlier_t)
+    match_ref[...] = jnp.transpose(match_t)
+    slot_ref[...] = jnp.where(near_t > 0.0, before_t, float(SLOTS))
+    all_lanes = lax.broadcasted_iota(jnp.int32, (DEVS, DEVS), 1)
+    permute[...] = jnp.where(expert[:, 0:1] == all_lanes, 1.0, 0.0).astype(jnp.bfloat16)
     for c in range(SLOTS):
-        select[c * DEVS : (c + 1) * DEVS, :] = jnp.transpose(
-            jnp.where(before == float(c), match, 0.0)
-        ).astype(jnp.bfloat16)
-
-    for t in range(2):
-        arrived_in(block(t, 3, 0), first_in.at[t, 0])
-        push(part(block(t, 3, 0), 0), part(block(t, 3, 0), 0), t, 1, 0, gather_out, first_in.at[t, 2])
-        pass_on(t, 3, block(t, 3, 0))
-        arrived_in(block(t, 1, 0), first_in.at[t, 1])
-        push(part(block(t, 1, 0), 1), part(block(t, 1, 0), 1), t, 3, 0, gather_out, first_in.at[t, 3])
-        pass_on(t, 1, block(t, 1, 0))
-    for t in range(2):
-        arrived_in(part(block(t, 2, 0), 0), first_in.at[t, 2])
-        arrived_in(part(block(t, 2, 0), 1), first_in.at[t, 3])
-        pass_on(t, 2, block(t, 2, 0))
-
-    own.wait()
-    for i in range(5):
-        loads[i].wait()
-    weights_in = (w_query, w_key, w_value, w_gate)
-
-    def project_line(t, second):
-        heads = [head_at(t, first, second) for first in range(4)]
-        total = None
-        pieces = []
-        for h in heads:
-            piece = gathered[h, t].astype(jnp.float32)
-            square = piece * piece
-            total = square if total is None else total + square
-            pieces.append((piece * attn_gain[pl.ds(h, 1), :]).astype(jnp.bfloat16))
-        if second == 0:
-            squares[t] = total
-        else:
-            squares[t] += total
-        line = jnp.concatenate(pieces, axis=1)
-        for i, weight in enumerate(weights_in):
-            deep = jnp.concatenate(
-                [weight[pl.ds(pl.multiple_of(h * 128, 128), 128), :] for h in heads], axis=0
-            )
-            product = dot(line, deep)
-            if second == 0:
-                acc[t, :, i * HERE : (i + 1) * HERE] = product
-            else:
-                acc[t, :, i * HERE : (i + 1) * HERE] += product
-
-    def forward_line(t):
-        for first in (0, 3, 1, 2):
+        select[c * DEVS : (c + 1) * DEVS, :] = jnp.where(before_t == float(c), near_t, 0.0).astype(
+            jnp.bfloat16
+        )
+
+    for first in (3, 1, 2):
+        for t in range(2):
+            arrived_in(block(t, first, 0), first_in.at[t, first])
+            pass_on(t, first, block(t, first, 0))
+
+    def forward_line(first):
+        for t in range(2):
             lower = block(t, first, 3)
             arrived_in(lower, second_in.at[t, first, 0])
             push(part(lower, 0), part(lower, 0), t, 0, 1, gather_out, second_in.at[t, first, 2])
@@ -260,18 +234,52 @@
             arrived_in(upper, second_in.at[t, first, 1])
             push(part(upper, 1), part(upper, 1), t, 0, 3, gather_out, second_in.at[t, first, 3])
 
+    forward_line(0)
+    own.wait()
+    for i in range(5):
+        loads[i].wait()
+    weights_in = (w_query, w_key, w_value, w_gate)
+
+    def project_line(t, second, which=(0, 1, 2, 3)):
+        heads = [head_at(t, first, second) for first in range(4)]
+        total = None
+        pieces = []
+        for h in heads:
+            piece = gathered[h, t].astype(jnp.float32)
+            if 1 in which:
+                square = piece * piece
+                total = square if total is None else total + square
+            pieces.append((piece * attn_gain[pl.ds(h, 1), :]).astype(jnp.bfloat16))
+        if 1 in which:
+            if second == 0:
+                squares[t] = total
+            else:
+                squares[t] += total
+        gained = jnp.concatenate(pieces, axis=1)
+        for i in which:
+            weight = weights_in[i]
+            deep = jnp.concatenate(
+                [weight[pl.ds(pl.multiple_of(h * 128, 128), 128), :] for h in heads], axis=0
+            )
+            product = dot(gained, deep)
+            if second == 0:
+                acc[t, :, i * HERE : (i + 1) * HERE] = product
+            else:
+                acc[t, :, i * HERE : (i + 1) * HERE] += product
+
     project_line(0, 0)
     project_line(1, 0)
-    forward_line(0)
-    forward_line(1)
+    for first in (3, 1, 2):
+        forward_line(first)
     for t in range(2):
         project_line(t, 3)
         project_line(t, 1)
     for t in range(2):
-        for first in (0, 3, 1, 2):
+        for first in range(4):
             arrived_in(part(block(t, first, 2), 0), second_in.at[t, first, 2])
             arrived_in(part(block(t, first, 2), 1), second_in.at[t, first, 3])
-        project_line(t, 2)
+    for t in range(2):
+        project_line(t, 2, (1, 2))
 
     def scale_of(t):
         mean_sq = jnp.sum(squares[t], axis=-1, keepdims=True) * (1.0 / WIDTH)
@@ -298,6 +306,8 @@
         device_id_type=MESH,
     )
     pair.start()
+    project_line(0, 2, (0, 3))
+    project_line(1, 2, (0, 3))
 
     causal = lax.broadcasted_iota(jnp.int32, (BLOCK, BLOCK), 0) >= lax.broadcasted_iota(
         jnp.int32, (BLOCK, BLOCK), 1
@@ -316,6 +326,7 @@
             )
             scores = jnp.where(causal, scores, 0.0).astype(jnp.bfloat16)
             mixed[t, :, cols] = dot(scores, values[t, :, cols])
+        acc[t, :, 3 * HERE : 4 * HERE] = jax.nn.sigmoid(acc[t, :, 3 * HERE : 4 * HERE] * scale_of(t))
 
     pair.wait_recv()
     total_out[...] = (states[my_core] + pair_in[...].astype(jnp.float32)).astype(jnp.bfloat16)
@@ -356,7 +367,7 @@
     hand_over.wait_recv()
 
     for t in range(2):
-        gate = jax.nn.sigmoid(acc[t, :, 3 * HERE : 4 * HERE] * scale_of(t))
+        gate = acc[t, :, 3 * HERE : 4 * HERE]
         for h in range(2):
             cols = slice(h * DH, (h + 1) * DH)
             prefix = jnp.where(my_core == t, prefix_out[1, h], prefix_in[h])
@@ -401,41 +412,26 @@
                 + r2[t, k, 0].astype(jnp.float32)
                 + r2[t, k, 1].astype(jnp.float32)
             )
-            if k == 2:
-                s3[t, 0] = line_sum[:, :PIECE].astype(jnp.bfloat16)
-                push(s3.at[t, 0], r3.at[t, 0], t, 1, 0, sum_out.at[2], sum3_in.at[t, 0])
-                s3[t, 1] = line_sum[:, PIECE:].astype(jnp.bfloat16)
-                push(s3.at[t, 1], r3.at[t, 1], t, 3, 0, sum_out.at[2], sum3_in.at[t, 1])
+            if k == 0:
+                near_sum[t] = line_sum
             else:
-                near_sum[t, k] = line_sum
-    for t in range(2):
-        arrived_in(r3.at[t, 0], sum3_in.at[t, 0])
-        s4[t, 0, :, 0:PIECE] = (
-            near_sum[t, 1, :, 0:PIECE] + r3[t, 0].astype(jnp.float32)
-        ).astype(jnp.bfloat16)
-        s4[t, 0, :, PIECE:WIDE] = near_sum[t, 1, :, PIECE:WIDE].astype(jnp.bfloat16)
-        push(s4.at[t, 0], r4.at[t, 0], t, 1, 0, sum_out.at[3], sum4_in.at[t, 0])
-        arrived_in(r3.at[t, 1], sum3_in.at[t, 1])
-        s4[t, 1, :, 0:PIECE] = near_sum[t, 3, :, 0:PIECE].astype(jnp.bfloat16)
-        s4[t, 1, :, PIECE:WIDE] = (
-            near_sum[t, 3, :, PIECE:WIDE] + r3[t, 1].astype(jnp.float32)
-        ).astype(jnp.bfloat16)
-        push(s4.at[t, 1], r4.at[t, 1], t, 3, 0, sum_out.at[3], sum4_in.at[t, 1])
+                s3[t, k - 1] = line_sum.astype(jnp.bfloat16)
+                push(s3.at[t, k - 1], r3.at[t, k - 1], t, k, 0, sum_out.at[2], sum3_in.at[t, k - 1])
     own_start = pl.multiple_of(lax.rem(my_head, 8) * ROWS, ROWS)
     for j in range(TILES):
-        residual_ref[:, j * 128 : (j + 1) * 128] = gathered[
+        residual_ref[0, :, j * 128 : (j + 1) * 128] = gathered[
             j, my_head // 8, pl.ds(own_start, ROWS), :
         ].astype(jnp.float32)
     for t in range(2):
-        arrived_in(r4.at[t, 0], sum4_in.at[t, 0])
-        arrived_in(r4.at[t, 1], sum4_in.at[t, 1])
-        residual_ref[:, t * WIDE : (t + 1) * WIDE] += (
-            near_sum[t, 0] + r4[t, 0].astype(jnp.float32) + r4[t, 1].astype(jnp.float32)
-        )
+        total = near_sum[t]
+        for k in range(3):
+            arrived_in(r3.at[t, k], sum3_in.at[t, k])
+            total = total + r3[t, k].astype(jnp.float32)
+        residual_ref[0, :, t * WIDE : (t + 1) * WIDE] += total
 
     for i in (8, 9):
         loads[i].wait()
-    moe_in = rms_scale(residual_ref[...], moe_gain[...]).astype(jnp.bfloat16)
+    moe_in = rms_scale(residual_ref[0], moe_gain[...]).astype(jnp.bfloat16)
     for j in range(0, TILES, 2):
         picked = dot(select[...], moe_in[:, j * 128 : (j + 2) * 128])
         for c in range(SLOTS):
@@ -443,57 +439,58 @@
                 spread[pl.ds(c * TILES + j + half, DEVS, CHUNK), :] = picked[
                     c * DEVS : (c + 1) * DEVS, half * 128 : (half + 1) * 128
                 ]
-    for o in range(SEQ):
-        to_seq = lax.rem(my_seq + o, SEQ)
-        start = pl.multiple_of(to_seq * (HEAD * CHUNK), HEAD * CHUNK)
-        outgoing[pl.ds(to_seq * HEAD, HEAD)] = (
-            spread[pl.ds(start, HEAD * CHUNK), :].astype(jnp.bfloat16).reshape(HEAD, CHUNK, 128)
+    def away(n, sign):
+        i = lax.rem(n, 4)
+        o = lax.rem(n // 4, SEQ)
+        dy = lax.rem(i + n // MEMBERS, 4)
+        x = lax.rem(my_x + 4 + sign * i, 4)
+        y = lax.rem(my_y + 4 + sign * dy, 4)
+        return (lax.rem(my_seq + SEQ + sign * o, SEQ), y * 4 + x)
+
+    part_lines = MEMBERS * CHUNK
+    for g in range(GROUPS):
+        members = pl.ds(g * MEMBERS, MEMBERS)
+        outgoing[members] = (
+            spread[g * part_lines : (g + 1) * part_lines, :]
+            .astype(jnp.bfloat16)
+            .reshape(MEMBERS, CHUNK, 128)
         )
-
-        def send(i, carry):
-            to_head = lax.rem(my_head + i, HEAD)
+        if g == 0:
+            pltpu.make_async_copy(outgoing.at[0], arrived.at[0], in_sem.at[0]).start()
+
+        def send(n, carry):
             pltpu.make_async_remote_copy(
-                src_ref=outgoing.at[to_seq * HEAD + to_head],
-                dst_ref=arrived.at[o * HEAD + my_head],
+                src_ref=outgoing.at[n],
+                dst_ref=arrived.at[n],
                 send_sem=out_sem,
-                recv_sem=in_sem.at[o],
-                device_id=(to_seq, to_head),
+                recv_sem=in_sem.at[g],
+                device_id=away(n, 1),
                 device_id_type=MESH,
             ).start()
             return carry
 
-        if o == 0:
-            pltpu.make_async_copy(outgoing.at[me], arrived.at[my_head], in_sem.at[0]).start()
-        lax.fori_loop(1 if o == 0 else 0, HEAD, send, 0)
+        lax.fori_loop(max(1, g * MEMBERS), (g + 1) * MEMBERS, send, 0)
 
     logits = dot(moe_in, w_router[...])
     scores = match_ref[...] * jax.nn.sigmoid(logits)
-    weights = scores / jnp.sum(scores, axis=1, keepdims=True)
-    before = before_ref[...]
-    spread_weights = jnp.concatenate(
-        [jnp.where(before == float(c), weights, 0.0) for c in range(SLOTS)], axis=1
-    )
-    high = spread_weights.astype(jnp.bfloat16)
-    low = (spread_weights - high.astype(jnp.float32)).astype(jnp.bfloat16)
-    combine = jnp.concatenate([high, low], axis=0)
+    weights = jnp.transpose(scores / jnp.sum(scores, axis=1, keepdims=True))
+    high = weights.astype(jnp.bfloat16)
+    low = (weights - high.astype(jnp.float32)).astype(jnp.bfloat16)
+    near_high = dot(permute[...], high)
+    near_low = dot(permute[...], low)
 
     for i in (10, 11, 12):
         loads[i].wait()
-    part_rows = HALF * SLOTS
-    for p in range(2):
-        for o in range(p * SEQ // 2, (p + 1) * SEQ // 2):
-            group = arrived.at[pl.ds(o * HEAD, HEAD)]
-            arrived_in(group, in_sem.at[o])
-        for q in range(4):
-            chunk = arrived[pl.ds(p * HALF + q * HEAD, HEAD)]
-            spread[pl.ds(q * HEAD * CHUNK, HEAD * CHUNK), :] = chunk.astype(jnp.float32).reshape(
-                HEAD * CHUNK, 128
+    part_rows = MEMBERS * SLOTS
+    for g in range(GROUPS):
+        members = pl.ds(g * MEMBERS, MEMBERS)
+        arrived_in(arrived.at[members], in_sem.at[g])
+        spread[0:part_lines, :] = arrived[members].astype(jnp.float32).reshape(part_lines, 128)
+        for j in range(TILES):
+            rows[:, j * 128 : (j + 1) * 128] = spread[pl.ds(j, part_rows, TILES), :].astype(
+                jnp.bfloat16
             )
-        for j in range(TILES):
-            rows[0:part_rows, j * 128 : (j + 1) * 128] = spread[
-                pl.ds(j, part_rows, TILES), :
-            ].astype(jnp.bfloat16)
-        inputs = rows[0:part_rows, :]
+        inputs = rows[...]
         hidden = (jax.nn.silu(dot(inputs, gate_w[...])) * dot(inputs, up_w[...])).astype(
             jnp.bfloat16
         )
@@ -503,43 +500,52 @@
                 spread[pl.ds(j + half, part_rows, TILES), :] = produced[
                     :, half * 128 : (half + 1) * 128
                 ]
-        for o in range(p * SEQ // 2, (p + 1) * SEQ // 2):
-            q = o - p * SEQ // 2
-            result[pl.ds(o * HEAD, HEAD)] = (
-                spread[pl.ds(q * HEAD * CHUNK, HEAD * CHUNK), :]
-                .astype(jnp.bfloat16)
-                .reshape(HEAD, CHUNK, 128)
-            )
-            to_seq = lax.rem(my_seq + SEQ - o, SEQ)
-
-            def send_back(i, carry):
-                to_head = lax.rem(my_head + i, HEAD)
-                pltpu.make_async_remote_copy(
-                    src_ref=result.at[o * HEAD + to_head],
-                    dst_ref=returned.at[me],
-                    send_sem=back_out_sem,
-                    recv_sem=back_in_sem,
-                    device_id=(to_seq, to_head),
-                    device_id_type=MESH,
-                ).start()
-                return carry
-
-            if o == 0:
-                pltpu.make_async_copy(result.at[my_head], returned.at[me], back_in_sem).start()
-            lax.fori_loop(1 if o == 0 else 0, HEAD, send_back, 0)
-
-    arrived_in(returned, back_in_sem)
-    for q in range(SEQ):
-        spread[pl.ds(q * HEAD * CHUNK, HEAD * CHUNK), :] = (
-            returned[pl.ds(q * HEAD, HEAD)].astype(jnp.float32).reshape(HEAD * CHUNK, 128)
+        result[members] = (
+            spread[0:part_lines, :].astype(jnp.bfloat16).reshape(MEMBERS, CHUNK, 128)
         )
-    for c in range(SLOTS):
-        for j in range(TILES):
-            rows[c * DEVS : (c + 1) * DEVS, j * 128 : (j + 1) * 128] = spread[
-                pl.ds(c * TILES + j, DEVS, CHUNK), :
-            ].astype(jnp.bfloat16)
-    both = dot(combine, rows[...])
-    layer_out[0] = residual_ref[...] + both[:ROWS] + both[ROWS:]
+        if g == 0:
+            pltpu.make_async_copy(result.at[0], returned.at[0], back_in_sem.at[0]).start()
+
+        def send_back(n, carry):
+            pltpu.make_async_remote_copy(
+                src_ref=result.at[n],
+                dst_ref=returned.at[n],
+                send_sem=back_out_sem,
+                recv_sem=back_in_sem.at[g],
+                device_id=away(n, -1),
+                device_id_type=MESH,
+            ).start()
+            return carry
+
+        lax.fori_loop(max(1, g * MEMBERS), (g + 1) * MEMBERS, send_back, 0)
+
+    def over_rows(a, b):
+        return lax.dot_general(
+            a, b, (((0,), (0,)), ((), ())), preferred_element_type=jnp.float32
+        )
+
+    for g in range(GROUPS):
+        members = pl.ds(g * MEMBERS, MEMBERS)
+        arrived_in(returned.at[members], back_in_sem.at[g])
+        spread[0:part_lines, :] = returned[members].astype(jnp.float32).reshape(part_lines, 128)
+        for c in range(SLOTS):
+            for j in range(TILES):
+                rows[c * MEMBERS : (c + 1) * MEMBERS, j * 128 : (j + 1) * 128] = spread[
+                    pl.ds(c * TILES + j, MEMBERS, CHUNK), :
+                ].astype(jnp.bfloat16)
+        here = slice(g * MEMBERS, (g + 1) * MEMBERS)
+        slots = slot_ref[here, :]
+        parts = [
+            jnp.concatenate(
+                [jnp.where(slots == float(c), near[here, :], 0.0) for c in range(SLOTS)], axis=0
+            ).astype(jnp.bfloat16)
+            for near in (near_high, near_low)
+        ]
+        added = over_rows(parts[0], rows[...]) + over_rows(parts[1], rows[...])
+        if g == 0:
+            moe_ref[0] = added
+        else:
+            moe_ref[0] += added
 
     sent = gathered.at[pl.ds(0, HEAD - 1)]
     pltpu.make_async_copy(sent, sent, gather_out).wait()
@@ -547,7 +553,7 @@
     for total in totals:
         total.wait_send()
     hand_over.wait_send()
-    for i, ref in enumerate((s1, s2, s3, s4)):
+    for i, ref in enumerate((s1, s2, s3)):
         pltpu.make_async_copy(ref, ref, sum_out.at[i]).wait()
     sent = outgoing.at[pl.ds(0, DEVS - 1)]
     pltpu.make_async_copy(sent, sent, out_sem).wait()
@@ -582,7 +588,7 @@
         w_out,
         moe_gain.reshape(1, WIDTH),
         w_router,
-        expert_picks,
+        jnp.transpose(expert_picks, (0, 2, 1)),
         exp_gate[0],
         exp_up[0],
         exp_down[0],
@@ -597,11 +603,11 @@
     def sems(*shape):
         return pltpu.SemaphoreType.DMA(shape)
 
-    return pl.pallas_call(
+    residual, moe_out = pl.pallas_call(
         layer_kernel,
-        out_shape=jax.ShapeDtypeStruct((1, ROWS, WIDTH), jnp.float32),
+        out_shape=(jax.ShapeDtypeStruct((1, ROWS, WIDTH), jnp.float32),) * 2,
         in_specs=[pl.BlockSpec(memory_space=pl.ANY)] * len(args),
-        out_specs=pl.BlockSpec(memory_space=pltpu.VMEM),
+        out_specs=(pl.BlockSpec(memory_space=pltpu.VMEM),) * 2,
         scratch_shapes=[pltpu.VMEM(a.shape, a.dtype) for a in args[1:]]
         + [
             half(HEAD, 2, BLOCK, 128),
@@ -619,25 +625,23 @@
             full(2, BLOCK, HERE),
             half(2, BLOCK, HERE),
             full(2 * BLOCK, WIDTH),
-            full(2, 4, ROWS, WIDE),
+            full(2, ROWS, WIDE),
             half(2, 4, 2, ROWS, PIECE),
             half(2, 4, 2, ROWS, PIECE),
             half(2, 4, 2, ROWS, WIDE),
             half(2, 4, 2, ROWS, WIDE),
-            half(2, 2, ROWS, PIECE),
-            half(2, 2, ROWS, PIECE),
-            half(2, 2, ROWS, WIDE),
-            half(2, 2, ROWS, WIDE),
+            half(2, 3, ROWS, WIDE),
+            half(2, 3, ROWS, WIDE),
             half(DEVS * SLOTS, ROWS),
             full(ROWS, DEVS),
-            full(ROWS, DEVS),
-            full(ROWS, WIDTH),
+            half(DEVS, DEVS),
+            full(DEVS, ROWS),
             full(DEVS * CHUNK, 128),
             half(DEVS, CHUNK, 128),
             half(DEVS, CHUNK, 128),
             half(DEVS, CHUNK, 128),
             half(DEVS, CHUNK, 128),
-            half(DEVS * SLOTS, WIDTH),
+            half(MEMBERS * SLOTS, WIDTH),
             sems(13),
             sems(),
             sems(),
@@ -645,15 +649,14 @@
             sems(2, 4, 4),
             sems(5),
             sems(5),
-            sems(4),
+            sems(3),
             sems(2, 4, 2),
             sems(2, 4, 2),
-            sems(2, 2),
-            sems(2, 2),
+            sems(2, 3),
             sems(),
-            sems(SEQ),
+            sems(GROUPS),
             sems(),
-            sems(),
+            sems(GROUPS),
         ],
         compiler_params=pltpu.CompilerParams(
             collective_id=1, has_side_effects=True, vmem_limit_bytes=56 * 1024 * 1024
@@ -662,6 +665,7 @@
             flops=7 << 30, bytes_accessed=20 << 20, transcendentals=0
         ),
     )(*args)
+    return residual + moe_out
 
 
 def solution(mesh):

time: 99.5 us -> 90.5 us (0.910)
  Pallas kernels: 96.2 us -> 88.1 us
  local copies, waits for them, and re-layouts: 3.04 us -> 0 us
  other arithmetic: 0 us -> 1.76 us
    pallas_call x1, Pallas kernels: 96.2 us -> 88.1 us  [local(): pl.pallas_call(layer_kernel, out_shape=(jax.ShapeDtypeStruct((1, ROWS, WI...]
    unnamed x2 -> x0, local copies, waits for them, and re-layouts: 3.04 us -> none
    add x0 -> x1, other arithmetic: none -> 1.76 us  [local(): return residual + moe_out]
where the time goes in v3:
time: 90.5 us; the launch traced here: 89.9 us
  Pallas kernels  88.1 us (97%)
  other arithmetic  1.76 us (2%)
    pallas_call x1, Pallas kernels, local(): pl.pallas_call(layer_kernel, out_shape=(jax.ShapeDtypeStruct((1, ROWS, WI...  88.1 us

profile of v3, /device:TPU:1, one launch (start us, length us, event | category | flops | bytes accessed | tf_op | source)
XLA Modules:
  0.0 89.9 jit_solution(14293178407167820276)
XLA Ops:
  0.0 88.1 %shard_map.136 = (f32[1,32,2048]{2,1,0:T(8,128)}, f32[1,32,2048]{2,1,0:T(8,128)}) custom-call(bf16[2,256,128]{2,1,0:T(8,128)(2,1)} %tokens_hbm.1, f32[16,128]{1,0:T(8,128)} %bitcast.10, bf16[2048,256]{1,0:T(8,128)(2,1)} %query_hbm.1, bf16[2048,256]{1,0:T(8,128)(2,1)} %key_hbm.1, bf16[2048,256]{1,0:T(8,128)(2,1)} %value_hbm.1, bf16[2048,256]{1,0:T(8,128)(2,1)} %gate_hbm.1, ...), custom_call_target="tpu_custom_call" | custom-call | flops 7516192768 | bytes 20971520 | tf_op jit(solution)/shard_map/pallas_call | solution.py:606
  88.1 1.8 %add.3 = f32[1,32,2048]{2,1,0:T(8,128)} add(f32[1,32,2048]{2,1,0:T(8,128)} %get-tuple-element.7, f32[1,32,2048]{2,1,0:T(8,128)} %get-tuple-element.8) | non-fusion elementwise | flops 65536 | bytes 786432 | tf_op jit(solution)/shard_map/add | solution.py:668

commit v4 on v3

--- a/solution.py
+++ b/solution.py
@@ -199,7 +199,7 @@
     step_x = lax.rem(line, 4)
     expert_x = lax.rem(my_x + step_x, 4)
     expert_y = lax.rem(my_y + step_x + offset, 4)
-    expert_seq = lax.rem(my_seq + lax.rem(line // 4, SEQ), SEQ)
+    expert_seq = lax.rem(my_seq + lax.rem(line // 4 + 2 * step_x, SEQ), SEQ)
     expert = expert_seq * HEAD + expert_y * 4 + expert_x
     picks = picks_ref[0]
     match_t = jnp.zeros((DEVS, ROWS), jnp.float32)
@@ -215,10 +215,13 @@
     slot_ref[...] = jnp.where(near_t > 0.0, before_t, float(SLOTS))
     all_lanes = lax.broadcasted_iota(jnp.int32, (DEVS, DEVS), 1)
     permute[...] = jnp.where(expert[:, 0:1] == all_lanes, 1.0, 0.0).astype(jnp.bfloat16)
-    for c in range(SLOTS):
-        select[c * DEVS : (c + 1) * DEVS, :] = jnp.where(before_t == float(c), near_t, 0.0).astype(
-            jnp.bfloat16
-        )
+    for g in range(GROUPS):
+        here = slice(g * MEMBERS, (g + 1) * MEMBERS)
+        for c in range(SLOTS):
+            start = (g * SLOTS + c) * MEMBERS
+            select[start : start + MEMBERS, :] = jnp.where(
+                before_t[here, :] == float(c), near_t[here, :], 0.0
+            ).astype(jnp.bfloat16)
 
     for first in (3, 1, 2):
         for t in range(2):
@@ -306,8 +309,6 @@
         device_id_type=MESH,
     )
     pair.start()
-    project_line(0, 2, (0, 3))
-    project_line(1, 2, (0, 3))
 
     causal = lax.broadcasted_iota(jnp.int32, (BLOCK, BLOCK), 0) >= lax.broadcasted_iota(
         jnp.int32, (BLOCK, BLOCK), 1
@@ -343,8 +344,9 @@
     ]
     for total in totals:
         total.start()
-    inner(0)
-    inner(1)
+    for t in range(2):
+        project_line(t, 2, (0, 3))
+        inner(t)
     base = jnp.zeros((2, DH, DH), jnp.float32)
     for dz in (1, 2, 3):
         totals[dz - 1].wait_recv()
@@ -432,16 +434,9 @@
     for i in (8, 9):
         loads[i].wait()
     moe_in = rms_scale(residual_ref[0], moe_gain[...]).astype(jnp.bfloat16)
-    for j in range(0, TILES, 2):
-        picked = dot(select[...], moe_in[:, j * 128 : (j + 2) * 128])
-        for c in range(SLOTS):
-            for half in range(2):
-                spread[pl.ds(c * TILES + j + half, DEVS, CHUNK), :] = picked[
-                    c * DEVS : (c + 1) * DEVS, half * 128 : (half + 1) * 128
-                ]
     def away(n, sign):
         i = lax.rem(n, 4)
-        o = lax.rem(n // 4, SEQ)
+        o = lax.rem(n // 4 + 2 * i, SEQ)
         dy = lax.rem(i + n // MEMBERS, 4)
         x = lax.rem(my_x + 4 + sign * i, 4)
         y = lax.rem(my_y + 4 + sign * dy, 4)
@@ -450,6 +445,14 @@
     part_lines = MEMBERS * CHUNK
     for g in range(GROUPS):
         members = pl.ds(g * MEMBERS, MEMBERS)
+        chosen = select[g * MEMBERS * SLOTS : (g + 1) * MEMBERS * SLOTS, :]
+        for j in range(0, TILES, 2):
+            picked = dot(chosen, moe_in[:, j * 128 : (j + 2) * 128])
+            for c in range(SLOTS):
+                for half in range(2):
+                    spread[pl.ds(g * part_lines + c * TILES + j + half, MEMBERS, CHUNK), :] = picked[
+                        c * MEMBERS : (c + 1) * MEMBERS, half * 128 : (half + 1) * 128
+                    ]
         outgoing[members] = (
             spread[g * part_lines : (g + 1) * part_lines, :]
             .astype(jnp.bfloat16)
@@ -506,7 +509,8 @@
         if g == 0:
             pltpu.make_async_copy(result.at[0], returned.at[0], back_in_sem.at[0]).start()
 
-        def send_back(n, carry):
+        def send_back(m, carry):
+            n = (2 * g + 1) * MEMBERS - 1 - m + (1 if g == 0 else 0)
             pltpu.make_async_remote_copy(
                 src_ref=result.at[n],
                 dst_ref=returned.at[n],

time: 90.5 us -> 88.2 us (0.975)
  Pallas kernels: 88.1 us -> 86.3 us
    pallas_call x1, Pallas kernels: 88.1 us -> 86.3 us  [local(): pl.pallas_call(layer_kernel, out_shape=(jax.ShapeDtypeStruct((1, ROWS, WI...]
where the time goes in v4:
time: 88.2 us; the launch traced here: 88.1 us
  Pallas kernels  86.3 us (98%)
  other arithmetic  1.76 us (2%)
    pallas_call x1, Pallas kernels, local(): pl.pallas_call(layer_kernel, out_shape=(jax.ShapeDtypeStruct((1, ROWS, WI...  86.3 us

profile of v4, /device:TPU:1, one launch (start us, length us, event | category | flops | bytes accessed | tf_op | source)
XLA Modules:
  0.0 88.1 jit_solution(11700900179460818208)
XLA Ops:
  0.0 86.3 %shard_map.136 = (f32[1,32,2048]{2,1,0:T(8,128)}, f32[1,32,2048]{2,1,0:T(8,128)}) custom-call(bf16[2,256,128]{2,1,0:T(8,128)(2,1)} %tokens_hbm.1, f32[16,128]{1,0:T(8,128)} %bitcast.10, bf16[2048,256]{1,0:T(8,128)(2,1)} %query_hbm.1, bf16[2048,256]{1,0:T(8,128)(2,1)} %key_hbm.1, bf16[2048,256]{1,0:T(8,128)(2,1)} %value_hbm.1, bf16[2048,256]{1,0:T(8,128)(2,1)} %gate_hbm.1, ...), custom_call_target="tpu_custom_call" | custom-call | flops 7516192768 | bytes 20971520 | tf_op jit(solution)/shard_map/pallas_call | solution.py:610
  86.3 1.8 %add.3 = f32[1,32,2048]{2,1,0:T(8,128)} add(f32[1,32,2048]{2,1,0:T(8,128)} %get-tuple-element.7, f32[1,32,2048]{2,1,0:T(8,128)} %get-tuple-element.8) | non-fusion elementwise | flops 65536 | bytes 786432 | tf_op jit(solution)/shard_map/add | solution.py:672

commit v5 on v4

--- a/solution.py
+++ b/solution.py
@@ -56,7 +56,6 @@
     exp_gate_hbm,
     exp_up_hbm,
     exp_down_hbm,
-    residual_ref,
     moe_ref,
     attn_gain,
     w_query,
@@ -97,6 +96,7 @@
     match_ref,
     permute,
     slot_ref,
+    residual_ref,
     spread,
     outgoing,
     arrived,
@@ -547,7 +547,7 @@
         ]
         added = over_rows(parts[0], rows[...]) + over_rows(parts[1], rows[...])
         if g == 0:
-            moe_ref[0] = added
+            moe_ref[0] = residual_ref[0] + added
         else:
             moe_ref[0] += added
 
@@ -607,11 +607,11 @@
     def sems(*shape):
         return pltpu.SemaphoreType.DMA(shape)
 
-    residual, moe_out = pl.pallas_call(
+    (out,) = pl.pallas_call(
         layer_kernel,
-        out_shape=(jax.ShapeDtypeStruct((1, ROWS, WIDTH), jnp.float32),) * 2,
+        out_shape=(jax.ShapeDtypeStruct((1, ROWS, WIDTH), jnp.float32),),
         in_specs=[pl.BlockSpec(memory_space=pl.ANY)] * len(args),
-        out_specs=(pl.BlockSpec(memory_space=pltpu.VMEM),) * 2,
+        out_specs=(pl.BlockSpec(memory_space=pltpu.VMEM),),
         scratch_shapes=[pltpu.VMEM(a.shape, a.dtype) for a in args[1:]]
         + [
             half(HEAD, 2, BLOCK, 128),
@@ -640,6 +640,7 @@
             full(ROWS, DEVS),
             half(DEVS, DEVS),
             full(DEVS, ROWS),
+            full(1, ROWS, WIDTH),
             full(DEVS * CHUNK, 128),
             half(DEVS, CHUNK, 128),
             half(DEVS, CHUNK, 128),
@@ -669,7 +670,7 @@
             flops=7 << 30, bytes_accessed=20 << 20, transcendentals=0
         ),
     )(*args)
-    return residual + moe_out
+    return out
 
 
 def solution(mesh):

time: 88.2 us -> 88.1 us (level)
  other arithmetic: 1.76 us -> 0 us
  local copies, waits for them, and re-layouts: 0 us -> 1.67 us
    add x1 -> x0, other arithmetic: 1.76 us -> none  [local(): return residual + moe_out]
    unnamed x0 -> x1, local copies, waits for them, and re-layouts: none -> 1.67 us
where the time goes in v5:
time: 88.1 us; the launch traced here: 88 us
  Pallas kernels  86.3 us (98%)
  local copies, waits for them, and re-layouts  1.67 us (2%)
    pallas_call x1, Pallas kernels, local(): pl.pallas_call(layer_kernel, out_shape=(jax.ShapeDtypeStruct((1, ROWS, WI...  86.3 us

profile of v5, /device:TPU:1, one launch (start us, length us, event | category | flops | bytes accessed | tf_op | source)
XLA Modules:
  0.0 88.0 jit_solution(13153295013887486384)
XLA Ops:
  0.0 86.3 %shard_map.136 = f32[1,32,2048]{2,1,0:T(8,128)} custom-call(bf16[2,256,128]{2,1,0:T(8,128)(2,1)} %tokens_hbm.1, f32[16,128]{1,0:T(8,128)} %bitcast.10, bf16[2048,256]{1,0:T(8,128)(2,1)} %query_hbm.1, bf16[2048,256]{1,0:T(8,128)(2,1)} %key_hbm.1, bf16[2048,256]{1,0:T(8,128)(2,1)} %value_hbm.1, bf16[2048,256]{1,0:T(8,128)(2,1)} %gate_hbm.1, ...), custom_call_target="tpu_custom_call" | custom-call | flops 7516192768 | bytes 20971520 | tf_op jit(solution)/shard_map/pallas_call | solution.py:610
  86.3 1.7 %copy.16 = f32[1,32,2048]{2,1,0:T(8,128)} copy(f32[1,32,2048]{2,1,0:T(8,128)} %shard_map.136) | data formatting | bytes 524288
